TPU v7x, 128 devices: a whole 4x4x4 slice. The times are simulated.
128 devices in a mesh: ta: 32 (over z, y_lo, x), ba: 4 (over y_hi, core).
Axes of the slice: x: 4, y: 4 (y_hi: 2, y_lo: 2; y = y_hi * 2 + y_lo), z: 4, core: 2. Of those that a mesh axis runs over, the one named last changes fastest.
Arguments:
- samples: int32 [1048576, 512], P('ta', 'ba'), may hold values from -128 to 127
- input_gain: float32 [512], P('ba'), may hold values from 0.005 to 0.03
- pfb_weights: float32 [16, 1024], replicated, may hold values from -1.5 to 1.5
- chan_map: int32 [512], replicated, may hold values from 0 to 511, each once
Outputs:
- visibility: float32 [2, 512, 512, 512], P(None, ('ta', 'ba'))
Inputs may be any that keep to these rules, and one draw needn't show every extreme that they name: `chan_map`: each of the 512 channel numbers appears exactly once.
All inputs are finite; a program needn't handle non-finite values.
Results may differ from a plain program's by a relative error of at most 0.0036.
Values may be sent and summed in bfloat16 or wider, within the bound.
No kernel may reach another device: no remote copies, remote signals or barrier semaphores. Data moves between devices by JAX's collectives and lax.ppermute only.
A program may use at most 128 MiB of HBM per device.

v0:
```python
import math

import jax
import jax.numpy as jnp
from jax import lax
from jax.sharding import PartitionSpec as P


def from_behind(block, axis, distance):
    devices = range(lax.axis_size(axis))
    route = [(i - distance, i) for i in devices if i - distance in devices]
    return lax.ppermute(block, axis, route)


def build_table(chan_map, frame_len):
    sample_idx = jnp.arange(frame_len, dtype=jnp.int32)
    product = sample_idx[:, None] * chan_map[None, :] % frame_len
    angle = product.astype(jnp.float32) * (2.0 * math.pi / frame_len)
    scale = 1.0 / math.sqrt(frame_len)
    stacked = jnp.stack([jnp.cos(angle) * scale, -jnp.sin(angle) * scale], axis=-1)
    return stacked.reshape(frame_len, -1).astype(jnp.bfloat16)


def rotate_pair(values):
    return jnp.stack([values[..., 1], -values[..., 0]], axis=-1)


def per_device(samples, input_gain, pfb_weights, chan_map):
    tap_count = pfb_weights.shape[0]
    frame_len = pfb_weights.shape[1]
    row_count, inputs_dev = samples.shape
    spectra_dev = row_count // frame_len
    calibrated = (samples.astype(jnp.float32) * input_gain[None, :]).astype(jnp.bfloat16)
    frames = calibrated.reshape(spectra_dev, frame_len, inputs_dev)
    history = from_behind(frames[spectra_dev - (tap_count - 1) :], "ta", 1)
    weights = pfb_weights[:, :, None]
    extended = jnp.concatenate([history, frames], axis=0)
    running = jnp.zeros((spectra_dev, frame_len, inputs_dev), jnp.float32)
    for tap_index in range(tap_count):
        running = running + weights[tap_index] * extended[
            tap_index : tap_index + spectra_dev
        ].astype(jnp.float32)
    filtered = running.astype(jnp.bfloat16)
    dft_table = build_table(chan_map, frame_len)
    spectra = jnp.einsum(
        "sni,nk->sik", filtered, dft_table, preferred_element_type=jnp.float32
    ).astype(jnp.bfloat16)
    turned = lax.all_to_all(
        lax.all_to_all(spectra, "ta", split_axis=2, concat_axis=0, tiled=True),
        "ba",
        split_axis=2,
        concat_axis=1,
        tiled=True,
    )
    total_spectra = turned.shape[0]
    cells = turned.reshape(total_spectra, turned.shape[1], turned.shape[2] // 2, 2)
    stacked = jnp.stack([cells, rotate_pair(cells)], axis=0)
    products = jnp.einsum("osicp,sjcp->ocij", stacked, cells, preferred_element_type=jnp.float32)
    return products / total_spectra


def solution(mesh):
    placed = (P("ta", "ba"), P("ba"), P(), P())
    return jax.shard_map(
        per_device,
        mesh=mesh,
        in_specs=placed,
        out_specs=P(None, ("ta", "ba"), None, None),
        check_vma=False,
    )
```

profile of v0, /device:TPU:4, one launch (start us, length us, event | category | flops | bytes accessed | tf_op | source)
XLA Modules:
  0.0 469.7 jit_solution(15802464341823464569)
XLA Ops:
  0.0 6.8 %multiply_convert_fusion = bf16[32768,128]{1,0:T(8,128)(2,1)S(1)} fusion(s32[32768,128]{1,0:T(8,128)} %param.4, f32[128]{0:T(128)} %param.5), kind=kLoop, calls=%fused_computation.33 | loop fusion | flops 12582912 | bytes 25166336 | tf_op jit(solution)/shard_map/convert_element_type | solution.py:33
  6.8 0.0 copy-start
  6.8 3.4 copy-done
  10.2 0.0 copy-start.2
  10.2 2.0 slice.156
  12.2 6.2 %copy.33 = bf16[15,1024,128]{1,2,0:T(8,128)(2,1)} copy(bf16[15,1024,128]{2,1,0:T(8,128)(2,1)} %bitcast.57) | data formatting | bytes 7864320 | tf_op jit(solution)/shard_map/slice | solution.py:35
  18.4 3.1 collective-permute-start
  21.5 0.0 copy-done.2
  21.5 8.7 %multiply_convert_fusion.2 = (bf16[1024,512,1]{1,0,2:T(8,128)(2,1)S(1)}, bf16[1024,512,1]{1,0,2:T(8,128)(2,1)S(1)}) fusion(s32[512]{0:T(512)S(1)} %copy-done.2), kind=kLoop, calls=%fused_computation.65 | loop fusion | flops 9961472 | bytes 2099200 | tf_op jit(solution)/shard_map/convert
  30.2 0.2 pad_maximum_fusion.1
  30.4 4.0 copy.36
  34.4 2.7 convert_element_type.98
  37.2 0.0 copy-start.1
  37.2 12.0 %copy.34 = bf16[32,1024,128]{1,2,0:T(8,128)(2,1)} copy(bf16[32,1024,128]{2,1,0:T(8,128)(2,1)} %bitcast.53) | data formatting | bytes 16777216 | tf_op jit(solution)/shard_map/reshape | solution.py:34
  49.2 0.0 copy-done.1
  49.2 58.0 %collective-permute-done = bf16[15,1024,128]{1,2,0:T(8,128)(2,1)} collective-permute-done((bf16[15,1024,128]{1,2,0:T(8,128)(2,1)}, bf16[15,1024,128]{1,2,0:T(8,128)(2,1)}, u32[]{:S(2)}, u32[]{:S(2)}) %collective-permute-start) | collective-permute-done | bytes 3932192 | tf_op jit(solution)/shard_map/ppermute | solution.py:12
  107.3 57.1 %fusion.21 = bf16[32,128,1024]{2,1,0:T(8,128)(2,1)} fusion(bf16[32,1024,128]{1,2,0:T(8,128)(2,1)} %copy.34, bf16[15,1024,128]{1,2,0:T(8,128)(2,1)} %collective-permute-done, f32[1024]{0:T(1024)S(1)} %bitcast.72, f32[1024]{0:T(1024)S(1)} %bitcast.73, f32[1024]{0:T(1024)S(1)} %bitcast.59, f32[1024]{0:T(1024)S(1)} %bitcast.60, f32[1024]{0:T(1024)S(1)} %bitcast.61, ...), kind=kOutput, calls=%fused_computation.54 | convolution fusion | flops 8858370048 | bytes 22872064 | tf_op jit(solution)/shard_map/sni,nk->sik/dot_general | solution.py:45
  164.4 12.5 %copy.38 = bf16[32,128,1024]{1,0,2:T(8,128)(2,1)} copy(bf16[32,128,1024]{2,1,0:T(8,128)(2,1)} %fusion.21) | data formatting | bytes 16777216 | tf_op jit(solution)/shard_map/convert_element_type | solution.py:47
  176.9 103.0 %all_to_all.33 = bf16[32,128,1024]{1,0,2:T(8,128)(2,1)} all-to-all(bf16[32,128,1024]{1,0,2:T(8,128)(2,1)} %copy.38), channel_id=1, replica_groups=mesh['ta'=32,'ba'=4] {'ta'}, dimensions={2} | all-to-all | bytes 16777216 | tf_op jit(solution)/shard_map/all_to_all | solution.py:49
  279.9 10.7 %copy.40 = bf16[32,32,128,32]{2,3,1,0:T(8,128)(2,1)} copy(bf16[32,32,128,32]{2,1,3,0:T(8,128)(2,1)} %bitcast.54) | data formatting | bytes 16777216 | tf_op jit(solution)/shard_map/all_to_all | solution.py:49
  290.6 9.8 %copy.41 = bf16[1024,128,32]{1,0,2:T(8,128)(2,1)} copy(bf16[1024,128,32]{1,2,0:T(8,128)(2,1)} %bitcast.55) | data formatting | bytes 16777216 | tf_op jit(solution)/shard_map/all_to_all | solution.py:49
  300.4 98.8 %all_to_all.34 = bf16[1024,128,32]{1,0,2:T(8,128)(2,1)S(1)} all-to-all(bf16[1024,128,32]{1,0,2:T(8,128)(2,1)} %copy.41), channel_id=1, replica_groups=mesh['ta'=32,'ba'=4] {'ba'}, dimensions={2} | all-to-all | bytes 16777216 | tf_op jit(solution)/shard_map/all_to_all | solution.py:48
  399.2 7.3 %copy.43 = bf16[1024,4,128,8]{2,1,0,3:T(4,128)(2,1)} copy(bf16[1024,4,128,8]{2,0,3,1:T(8,128)(2,1)S(1)} %bitcast.56) | data formatting | bytes 16777216 | tf_op jit(solution)/shard_map/all_to_all | solution.py:48
  406.5 13.1 %reshape.147 = bf16[1024,512,4,2]{1,0,3,2:T(8,128)(2,1)} reshape(bf16[1024,4,128,8]{2,1,0,3:T(4,128)(2,1)} %copy.43) | data formatting | bytes 16777216 | tf_op jit(solution)/shard_map/reshape | solution.py:56
  419.6 13.1 %stack_reshape.3 = bf16[1,1024,512,4,2]{2,1,4,0,3:T(8,128)(2,1)} reshape(bf16[1024,4,128,8]{2,1,0,3:T(4,128)(2,1)} %copy.43) | data formatting | bytes 16777216 | tf_op jit(solution)/shard_map/stack;reshape | solution.py:57
  432.8 5.0 %fusion.35 = (bf16[1024,512,4,1]{1,0,3,2:T(8,128)(2,1)S(1)}, bf16[1024,512,4,1]{1,0,3,2:T(8,128)(2,1)}) fusion(bf16[1024,512,4,2]{1,0,3,2:T(8,128)(2,1)} %reshape.147), kind=kLoop, calls=%fused_computation.71 | loop fusion | flops 2097152 | bytes 16777216 | tf_op jit(solution)/shard_map/slice | solution.py:25
  437.8 6.4 %maximum_bitcast_fusion = bf16[1,1024,512,4,2]{2,1,4,0,3:T(8,128)(2,1)} fusion(bf16[1024,512,4,1]{1,0,3,2:T(8,128)(2,1)} %get-tuple-element.6, bf16[1024,512,4,1]{1,0,3,2:T(8,128)(2,1)S(1)} %get-tuple-element.5), kind=kLoop, calls=%fused_computation.49 | loop fusion | flops 4194304 | bytes 16777216 | tf_op jit(solution)/shard_map/stack | solution.py:57
  444.2 15.7 %fusion.19 = f32[2,4,512,512]{2,3,0,1:T(8,128)} fusion(bf16[1,1024,512,4,2]{2,1,4,0,3:T(8,128)(2,1)} %maximum_bitcast_fusion, bf16[1,1024,512,4,2]{2,1,4,0,3:T(8,128)(2,1)} %stack_reshape.3, bf16[1024,512,4,2]{1,0,3,2:T(8,128)(2,1)} %reshape.147), kind=kOutput, calls=%fused_computation.52 | convolution fusion | flops 8625586176 | bytes 33554432 | tf_op jit(solution)/shard_map/osicp,sjcp->ocij/dot_general | solution.py:58
  459.9 9.9 %copy.46 = f32[2,4,512,512]{3,2,1,0:T(8,128)} copy(f32[2,4,512,512]{2,3,0,1:T(8,128)} %fusion.19) | data formatting | bytes 16777216 | tf_op jit(solution)/shard_map/div | solution.py:59
  (1 shorter events, 0.0 us)
Async XLA Ops:
  6.8 3.4 copy-start
  10.2 11.3 %copy-start.2 = (s32[512]{0:T(512)S(1)}, s32[512]{0:T(512)}, u32[]{:S(2)}) copy-start(s32[512]{0:T(512)} %param.7) | copy-start | bytes 6148
  18.4 88.9 %collective-permute-start = (bf16[15,1024,128]{1,2,0:T(8,128)(2,1)}, bf16[15,1024,128]{1,2,0:T(8,128)(2,1)}, u32[]{:S(2)}, u32[]{:S(2)}) collective-permute-start(bf16[15,1024,128]{1,2,0:T(8,128)(2,1)} %copy.33), channel_id=1, source_target_pairs={{0,4},{4,8},{8,12},{12,16},{16,20},{20,24},{24,28},{28,32},{32,36}... | collective-permute-start | bytes 11796488 | tf_op jit(solution)/shard_map/ppermute | solution.py:12
  37.2 12.0 %copy-start.1 = (f32[16,1024]{1,0:T(8,128)S(1)}, f32[16,1024]{1,0:T(8,128)}, u32[]{:S(2)}) copy-start(f32[16,1024]{1,0:T(8,128)} %param.6) | copy-start | bytes 196612
where the time goes:
time: 473 us; the launch traced here: 470 us
  blocking collectives  202 us (43%)
  local copies, waits for them, and re-layouts  107 us (23%)
  matrix products  72.8 us (15%)
  waiting for transfers between devices  58 us (12%)
  other arithmetic  27 us (6%)
    all_to_all x1, blocking collectives, per_device(): lax.all_to_all(spectra, 'ta', split_axis=2, concat_axis=0, tiled=True)  103 us
    all_to_all x1, blocking collectives, per_device(): lax.all_to_all(lax.all_to_all(spectra, 'ta', split_axis=2, concat_axis=0,...  98.8 us
    ppermute x1, waiting for transfers between devices, from_behind(): return lax.ppermute(block, axis, route)  58 us
    dot_general x1, matrix products, per_device(): jnp.einsum('sni,nk->sik', filtered, dft_table, preferred_element_type=jnp...  57.1 us
    all_to_all x2, local copies, waits for them, and re-layouts, per_device(): lax.all_to_all(spectra, 'ta', split_axis=2, concat_axis=0, tiled=True)  20.5 us
    dot_general x1, matrix products, per_device(): jnp.einsum('osicp,sjcp->ocij', stacked, cells, preferred_element_type=jnp...  15.7 us
    reshape x1, local copies, waits for them, and re-layouts, per_device(): turned.reshape(total_spectra, turned.shape[1], turned.shape[2] // 2, 2)  13.1 us
    another operation x1, local copies, waits for them, and re-layouts, per_device(): stacked = jnp.stack([cells, rotate_pair(cells)], axis=0)  13.1 us
  transfers between devices with their start and end apart: 1, of which 1 were waited for; matrix products, arithmetic and copies ran while one was open for 6% of the time, Pallas kernels for 0%

commit v1 on v0

v1 whole, which is shorter than its diff:
```python
import math

import jax
import jax.numpy as jnp
from jax import lax
from jax.sharding import PartitionSpec as P


def from_behind(block, axis, distance):
    devices = range(lax.axis_size(axis))
    route = [(i - distance, i) for i in devices if i - distance in devices]
    return lax.ppermute(block, axis, route)


def build_table(chan_map, frame_len):
    sample_idx = jnp.arange(frame_len, dtype=jnp.int32)
    product = chan_map[:, None] * sample_idx[None, :] % frame_len
    angle = product.astype(jnp.float32) * (2.0 * math.pi / frame_len)
    scale = 1.0 / math.sqrt(frame_len)
    stacked = jnp.stack([jnp.cos(angle) * scale, -jnp.sin(angle) * scale], axis=1)
    return stacked.reshape(-1, frame_len).astype(jnp.bfloat16)


def per_device(samples, input_gain, pfb_weights, chan_map):
    tap_count = pfb_weights.shape[0]
    frame_len = pfb_weights.shape[1]
    row_count, inputs_dev = samples.shape
    spectra_dev = row_count // frame_len
    times = lax.axis_size("ta")
    bands = lax.axis_size("ba")
    count = times * bands
    calibrated = (samples.astype(jnp.float32) * input_gain[None, :]).astype(jnp.bfloat16)
    frames = calibrated.reshape(spectra_dev, frame_len, inputs_dev)
    history = from_behind(frames[spectra_dev - (tap_count - 1) :], "ta", 1)
    weights = pfb_weights[:, :, None]
    extended = jnp.concatenate([history, frames], axis=0)
    running = jnp.zeros((spectra_dev, frame_len, inputs_dev), jnp.float32)
    for tap_index in range(tap_count):
        running = running + weights[tap_index] * extended[
            tap_index : tap_index + spectra_dev
        ].astype(jnp.float32)
    filtered = running.astype(jnp.bfloat16)
    dft_table = build_table(chan_map, frame_len)
    spectra = jnp.einsum(
        "kn,sni->ksi", dft_table, filtered, preferred_element_type=jnp.float32
    ).astype(jnp.bfloat16)
    columns = spectra.shape[0] // count
    turned = lax.all_to_all(
        spectra.reshape(count, columns, spectra_dev, inputs_dev), ("ta", "ba"), 0, 0, tiled=True
    )
    cells = turned.reshape(times, bands, columns // 2, 2, spectra_dev, inputs_dev)
    cells = cells.transpose(2, 3, 0, 4, 1, 5).reshape(
        columns // 2, 2, times * spectra_dev, bands * inputs_dev
    )
    rotated = jnp.stack([cells[:, 1], -cells[:, 0]], axis=1)
    real = jnp.einsum("cpsi,cpsj->cij", cells, cells, preferred_element_type=jnp.float32)
    imag = jnp.einsum("cpsi,cpsj->cij", rotated, cells, preferred_element_type=jnp.float32)
    return jnp.stack([real, imag]) / (times * spectra_dev)


def solution(mesh):
    placed = (P("ta", "ba"), P("ba"), P(), P())
    return jax.shard_map(
        per_device,
        mesh=mesh,
        in_specs=placed,
        out_specs=P(None, ("ta", "ba"), None, None),
        check_vma=False,
    )
```

time: 473 us -> 345 us (0.73)
  blocking collectives: 202 us -> 109 us
  local copies, waits for them, and re-layouts: 107 us -> 48.1 us
  other arithmetic: 27 us -> 75.7 us
  matrix products: 72.8 us -> 36 us
  waiting for transfers between devices: 58 us -> 72 us
    all_to_all x2 -> x1, blocking collectives: 202 us -> 109 us  [per_device(): lax.all_to_all(spectra.reshape(count, columns, spectra_dev, inputs_dev),...]
    dot_general x0 -> x1, other arithmetic: none -> 46.9 us  [per_device(): jnp.einsum('kn,sni->ksi', dft_table, filtered, preferred_element_type=jnp...]
    dot_general x2 -> x3, matrix products: 72.8 us -> 36 us  [the longest x1 14.3 us: per_device(): jnp.einsum('kn,sni->ksi', dft_table, filtered, preferred_element_type=jnp...]
    all_to_all x3 -> x0, local copies, waits for them, and re-layouts: 27.8 us -> none  [the longest x2 20.5 us: per_device(): lax.all_to_all(spectra, 'ta', split_axis=2, concat_axis=0, tiled=True)]
    another operation x2 -> x1, local copies, waits for them, and re-layouts: 17.1 us -> 2.16 us  [build_table(): jnp.stack([jnp.cos(angle) * scale, -jnp.sin(angle) * scale], axis=1)]
    ppermute x1, waiting for transfers between devices: 58 us -> 72 us  [from_behind(): return lax.ppermute(block, axis, route)]
    reshape x2 -> x3, local copies, waits for them, and re-layouts: 25.1 us -> 38.2 us  [the longest x1 16 us: per_device(): turned.reshape(times, bands, columns // 2, 2, spectra_dev, inputs_dev)]
    convert_element_type x2 -> x1, local copies, waits for them, and re-layouts: 15.2 us -> 2.29 us  [build_table(): return stacked.reshape(-1, frame_len).astype(jnp.bfloat16)]
  transfers between devices with their start and end apart: 1 -> 1, of which waited for: 1 -> 1; matrix products, arithmetic and copies ran while one was open for 6% -> 4% of each run, Pallas kernels for 0% -> 0%
where the time goes in v1:
time: 345 us
  blocking collectives  109 us (32%)
  other arithmetic  75.7 us (22%)
  waiting for transfers between devices  72 us (21%)
  local copies, waits for them, and re-layouts  48.1 us (14%)
  matrix products  36 us (10%)
    all_to_all x1, blocking collectives, per_device(): lax.all_to_all(spectra.reshape(count, columns, spectra_dev, inputs_dev),...  109 us
    ppermute x1, waiting for transfers between devices, from_behind(): return lax.ppermute(block, axis, route)  72 us
    dot_general x1, other arithmetic, per_device(): jnp.einsum('kn,sni->ksi', dft_table, filtered, preferred_element_type=jnp...  46.9 us
    reshape x1, local copies, waits for them, and re-layouts, per_device(): turned.reshape(times, bands, columns // 2, 2, spectra_dev, inputs_dev)  16 us
    dot_general x1, matrix products, per_device(): jnp.einsum('kn,sni->ksi', dft_table, filtered, preferred_element_type=jnp...  14.3 us
    reshape x1, local copies, waits for them, and re-layouts, per_device(): cells.transpose(2, 3, 0, 4, 1, 5)  13.1 us
    dot_general x1, matrix products, per_device(): jnp.einsum('cpsi,cpsj->cij', rotated, cells, preferred_element_type=jnp.f...  12.3 us
    dot_general x1, matrix products, per_device(): jnp.einsum('cpsi,cpsj->cij', cells, cells, preferred_element_type=jnp.flo...  9.44 us
  transfers between devices with their start and end apart: 1, of which 1 were waited for; matrix products, arithmetic and copies ran while one was open for 4% of the time, Pallas kernels for 0%

profile of v1, /device:TPU:4, one launch (start us, length us, event | category | flops | bytes accessed | tf_op | source)
XLA Modules:
  0.0 344.5 jit_solution(12805913838406242879)
XLA Ops:
  0.0 0.0 copy-start.3
  0.0 6.8 %multiply_convert_fusion = bf16[32768,128]{1,0:T(8,128)(2,1)S(1)} fusion(s32[32768,128]{1,0:T(8,128)} %param.4, f32[128]{0:T(128)} %param.5), kind=kLoop, calls=%fused_computation.29 | loop fusion | flops 12582912 | bytes 25166336 | tf_op jit(solution)/shard_map/convert_element_type | solution.py:32
  6.8 0.0 copy-start
  6.8 3.4 copy-done
  10.2 2.0 slice.156
  12.2 0.0 copy-start.2
  12.2 3.2 collective-permute-start
  15.4 0.0 copy-done.3
  15.4 9.1 %multiply_convert_fusion.2 = (bf16[512,1,1024]{2,0,1:T(8,128)(2,1)S(1)}, bf16[512,1,1024]{2,0,1:T(8,128)(2,1)S(1)}) fusion(s32[512]{0:T(512)S(1)} %copy-done.3), kind=kLoop, calls=%fused_computation.64 | loop fusion | flops 9961472 | bytes 2099200 | tf_op jit(solution)/shard_map/convert
  24.5 0.2 pad_maximum_fusion.1
  24.7 2.2 copy.16
  26.9 2.3 reshape.152
  29.2 0.0 copy-done.2
  29.2 72.0 %collective-permute-done = bf16[15,1024,128]{2,1,0:T(8,128)(2,1)} collective-permute-done((bf16[15,1024,128]{2,1,0:T(8,128)(2,1)}, bf16[15,1024,128]{2,1,0:T(8,128)(2,1)}, u32[]{:S(2)}, u32[]{:S(2)}) %collective-permute-start) | collective-permute-done | bytes 3932192 | tf_op jit(solution)/shard_map/ppermute | solution.py:12
  101.2 0.0 copy-start.1
  101.2 46.9 %add_convert_fusion.6 = bf16[32,1024,128]{2,1,0:T(8,128)(2,1)} fusion(bf16[32,1024,128]{2,1,0:T(8,128)(2,1)} %bitcast.39, bf16[15,1024,128]{2,1,0:T(8,128)(2,1)} %collective-permute-done, f32[1024]{0:T(1024)S(1)} %bitcast.56, f32[1024]{0:T(1024)S(1)} %bitcast.57, f32[1024]{0:T(1024)S(1)} %bitcast.43, f32[1024]{0:T(1024)S(1)} %bitcast.44, ...), kind=kLoop, calls=%fused_computation.28.clone.clone.clone.clone.1 | loop fusion | flops 264241152 | bytes 20774912 | tf_op jit(solution)/shard_map/kn,sni->ksi/dot_general | solution.py:44
  148.1 0.0 copy-done.1
  148.1 14.3 %convert_bitcast_fusion = bf16[128,8,32,128]{3,1,0,2:T(8,128)(2,1)} fusion(bf16[1024,1024,1]{1,0,2:T(8,128)(2,1)S(1)} %copy-done.1, bf16[32,1024,128]{2,1,0:T(8,128)(2,1)} %add_convert_fusion.6), kind=kOutput, calls=%fused_computation.51 | convolution fusion | flops 8594128896 | bytes 18874368 | tf_op jit(solution)/shard_map/kn,sni->ksi/dot_general | solution.py:44
  162.4 9.0 %copy.17 = bf16[128,8,32,128]{3,1,2,0:T(8,128)(2,1)} copy(bf16[128,8,32,128]{3,1,0,2:T(8,128)(2,1)} %convert_bitcast_fusion) | data formatting | bytes 16777216 | tf_op jit(solution)/shard_map/reshape | solution.py:49
  171.4 109.4 %all_to_all.5 = bf16[128,8,32,128]{3,1,2,0:T(8,128)(2,1)S(1)} all-to-all(bf16[128,8,32,128]{3,1,2,0:T(8,128)(2,1)} %copy.17), channel_id=1, replica_groups=mesh['ta'=32,'ba'=4] {'ta','ba'}, dimensions={0} | all-to-all | bytes 16777216 | tf_op jit(solution)/shard_map/all_to_all | solution.py:48
  280.8 16.0 %copy.26 = bf16[32,4,4,2,32,128]{5,1,4,0,3,2:T(4,128)(2,1)} copy(bf16[32,4,4,2,32,128]{5,3,2,4,1,0:T(2,128)(2,1)S(1)} %bitcast.40) | data formatting | bytes 16777216 | tf_op jit(solution)/shard_map/reshape | solution.py:51
  296.8 13.1 %reshape.151 = bf16[4,2,1024,512]{3,2,1,0:T(8,128)(2,1)} reshape(bf16[4,2,32,32,4,128]{5,4,3,2,1,0:T(4,128)(2,1)} %bitcast.41) | data formatting | bytes 16777216 | tf_op jit(solution)/shard_map/reshape | solution.py:52
  310.0 5.8 %fusion.30 = (bf16[4,1,1024,512]{3,2,1,0:T(8,128)(2,1)}, bf16[4,1,1024,512]{3,2,1,0:T(8,128)(2,1)}) fusion(bf16[4,2,1024,512]{3,2,1,0:T(8,128)(2,1)} %reshape.151), kind=kLoop, calls=%fused_computation.70 | loop fusion | flops 2097152 | bytes 16777216 | tf_op jit(solution)/shard_map/slice | solution.py:55
  315.8 9.4 %convolution_bitcast_fusion = f32[1,4,512,512]{3,2,1,0:T(8,128)S(1)} fusion(bf16[4,2,1024,512]{3,2,1,0:T(8,128)(2,1)} %reshape.151), kind=kOutput, calls=%fused_computation.58 | convolution fusion | flops 4294967296 | bytes 12582912 | tf_op jit(solution)/shard_map/cpsi,cpsj->cij/dot_general | solution.py:56
  325.2 12.3 %fusion.19 = f32[1,4,512,512]{3,2,1,0:T(8,128)} fusion(bf16[4,2,1024,512]{3,2,1,0:T(8,128)(2,1)} %reshape.151, bf16[4,1,1024,512]{3,2,1,0:T(8,128)(2,1)} %get-tuple-element.6, bf16[4,1,1024,512]{3,2,1,0:T(8,128)(2,1)} %get-tuple-element.5), kind=kOutput, calls=%fused_computation.57 | convolution fusion | flops 4299161600 | bytes 20971520 | tf_op jit(solution)/shard_map/cpsi,cpsj->cij/dot_general | solution.py:57
  337.6 6.9 %maximum_multiply_fusion = f32[2,4,512,512]{3,2,1,0:T(8,128)} fusion(f32[1,4,512,512]{3,2,1,0:T(8,128)} %fusion.19, f32[1,4,512,512]{3,2,1,0:T(8,128)S(1)} %convolution_bitcast_fusion), kind=kLoop, calls=%fused_computation.49 | loop fusion | flops 4194304 | bytes 16777216 | tf_op jit(solution)/shard_map/div | solution.py:58
  (1 shorter events, 0.0 us)
Async XLA Ops:
  0.0 15.4 %copy-start.3 = (s32[512]{0:T(512)S(1)}, s32[512]{0:T(512)}, u32[]{:S(2)}) copy-start(s32[512]{0:T(512)} %param.7) | copy-start | bytes 6148
  6.8 3.4 copy-start
  12.2 17.0 %copy-start.2 = (f32[16,1024]{1,0:T(8,128)S(1)}, f32[16,1024]{1,0:T(8,128)}, u32[]{:S(2)}) copy-start(f32[16,1024]{1,0:T(8,128)} %param.6) | copy-start | bytes 196612
  12.2 89.0 %collective-permute-start = (bf16[15,1024,128]{2,1,0:T(8,128)(2,1)}, bf16[15,1024,128]{2,1,0:T(8,128)(2,1)}, u32[]{:S(2)}, u32[]{:S(2)}) collective-permute-start(bf16[15,1024,128]{2,1,0:T(8,128)(2,1)} %bitcast.1), channel_id=1, source_target_pairs={{0,4},{4,8},{8,12},{12,16},{16,20},{20,24},{24,28},{28,32},{32,36}... | collective-permute-start | bytes 11796488 | tf_op jit(solution)/shard_map/ppermute | solution.py:12
  101.2 46.9 %copy-start.1 = (bf16[1024,1024,1]{1,0,2:T(8,128)(2,1)S(1)}, bf16[1024,1024,1]{1,0,2:T(8,128)(2,1)}, u32[]{:S(2)}) copy-start(bf16[1024,1024,1]{1,0,2:T(8,128)(2,1)} %reshape.152) | copy-start | bytes 6291460

commit v2 on v1

v2 whole, which is shorter than its diff:
```python
import functools
import math

import jax
import jax.numpy as jnp
import numpy as np
from jax import lax
from jax.experimental import pallas as pl
from jax.experimental.pallas import tpu as pltpu
from jax.sharding import PartitionSpec as P

LANES = 128
ROWS = 16
STEPS = 8
VMEM = 60 * 1024 * 1024
FILTER_COST = 1024


def build_table(channels, frame_len):
    turns = np.arange(channels)[:, None] * np.arange(frame_len)[None, :] % frame_len
    angle = turns * (2.0 * np.pi / frame_len)
    both = np.stack([np.cos(angle), -np.sin(angle)], axis=1) / math.sqrt(frame_len)
    return jnp.asarray(both.reshape(2 * channels, frame_len), dtype=jnp.bfloat16)


def calibrate_kernel(ahead, behind, first_ref, last_ref, gain_ref, head_ref, tail_ref):
    gain = gain_ref[...][None]
    own = last_ref.shape[0]
    head_ref[...] = (first_ref[...].astype(jnp.float32) * gain).astype(jnp.bfloat16)
    last = last_ref[own - behind :].astype(jnp.float32)
    tail_ref[...] = (last * gain).astype(jnp.bfloat16)


def calibrate_ends(frames, gain, ahead, behind):
    n_frames, frame_len, lanes = frames.shape
    part = frame_len // 4
    last = n_frames // ahead - 1
    return pl.pallas_call(
        functools.partial(calibrate_kernel, ahead, behind),
        grid=(4,),
        in_specs=[
            pl.BlockSpec((ahead, part, lanes), lambda j: (0, j, 0)),
            pl.BlockSpec((ahead, part, lanes), lambda j: (last, j, 0)),
            pl.BlockSpec((1, lanes), lambda j: (0, 0)),
        ],
        out_specs=[
            pl.BlockSpec((ahead, part, lanes), lambda j: (0, j, 0)),
            pl.BlockSpec((behind, part, lanes), lambda j: (0, j, 0)),
        ],
        out_shape=[
            jax.ShapeDtypeStruct((ahead, frame_len, lanes), jnp.bfloat16),
            jax.ShapeDtypeStruct((behind, frame_len, lanes), jnp.bfloat16),
        ],
        compiler_params=pltpu.CompilerParams(
            dimension_semantics=("arbitrary",), vmem_limit_bytes=VMEM
        ),
    )(frames, frames, gain)


def spectra_kernel(segments, taps, *refs):
    chan_ref, samples_ref, *halo_refs = refs[:-8]
    scale_ref, weight_ref, table, out_ref, part, weights, filtered, turned = refs[-8:]
    step = pl.program_id(0)
    spectra = sum(len(segment) - taps + 1 for segment in segments)
    part_rows = samples_ref.shape[1]
    columns = table.shape[0]
    pairs = spectra // 2

    @pl.when(step < STEPS)
    def _():
        weights[:, :taps] = weight_ref[...].T

        def tile(index, carry):
            row = pl.multiple_of(index * ROWS, ROWS)
            for half in range(2):
                rows = pl.ds(row + half * 8, 8)
                weight = [
                    jnp.broadcast_to(weights[rows, t : t + 1], (8, LANES)) for t in range(taps)
                ]
                base = 0
                for segment in segments:
                    count = len(segment) - taps + 1
                    sums = {}
                    for place, (source, frame, scale_row) in enumerate(segment):
                        if source == 0:
                            raw = samples_ref[frame, rows, :].astype(jnp.float32)
                            value = raw * scale_ref[scale_row : scale_row + 1, :]
                            value = value.astype(jnp.bfloat16).astype(jnp.float32)
                        else:
                            both = halo_refs[source - 1][frame, pl.ds(row, ROWS), :]
                            value = both.astype(jnp.float32)[half * 8 : half * 8 + 8]
                        for s in range(max(0, place - taps + 1), min(count, place + 1)):
                            term = value * weight[place - s]
                            sums[s] = sums[s] + term if s in sums else term
                        done = place - taps + 1
                        if done >= 0:
                            part[base + done, half * 8 : half * 8 + 8, :] = sums.pop(done)
                    base += count
            start = pl.multiple_of(step * part_rows + row, ROWS)
            for s in range(spectra):
                filtered[pl.ds(start, ROWS), s * LANES : (s + 1) * LANES] = part[s].astype(jnp.bfloat16)
            return carry

        lax.fori_loop(0, part_rows // ROWS, tile, 0)

    @pl.when(step >= STEPS)
    def _():
        pair = step - STEPS
        rhs = filtered[:, pl.ds(pl.multiple_of(pair * 2 * LANES, 2 * LANES), 2 * LANES)]
        block = 256
        for c in range(0, columns, block):
            product = jnp.dot(table[c : c + block, :], rhs, preferred_element_type=jnp.float32)
            for odd in range(2):
                turned[pl.ds(c * spectra + pair * 2 + odd, block, stride=spectra), :] = product[
                    :, odd * LANES : (odd + 1) * LANES
                ]

    @pl.when(step == STEPS + pairs - 1)
    def _():
        slots = out_ref.shape[1] // 2

        def emit(dest, carry):
            for slot in range(slots):
                rows = 2 * spectra
                first = chan_ref[dest * slots + slot] * rows
                values = turned[pl.ds(pl.multiple_of(first, rows), rows), :].astype(jnp.bfloat16)
                out_ref[dest, 2 * slot : 2 * slot + 2] = values.reshape(2, spectra, LANES)
            return carry

        lax.fori_loop(0, out_ref.shape[0], emit, 0)


def transform(segments, taps, dests, chan_map, samples, halos, scales, weights, table):
    n_frames, frame_len, lanes = samples.shape
    columns = table.shape[0]
    spectra = sum(len(segment) - taps + 1 for segment in segments)
    part_rows = frame_len // STEPS
    steps = STEPS + spectra // 2
    index = lambda j, chan: (0, jnp.minimum(j, STEPS - 1), 0)
    in_specs = [pl.BlockSpec((n_frames, part_rows, lanes), index)]
    in_specs += [pl.BlockSpec((halo.shape[0], part_rows, lanes), index) for halo in halos]
    in_specs += [
        pl.BlockSpec(scales.shape, lambda j, chan: (0, 0)),
        pl.BlockSpec((taps, part_rows), lambda j, chan: (0, jnp.minimum(j, STEPS - 1))),
        pl.BlockSpec(table.shape, lambda j, chan: (0, 0)),
    ]
    out_shape = (dests, 2 * chan_map.shape[0] // dests, spectra, lanes)
    return pl.pallas_call(
        functools.partial(spectra_kernel, segments, taps),
        grid_spec=pltpu.PrefetchScalarGridSpec(
            num_scalar_prefetch=1,
            grid=(steps,),
            in_specs=in_specs,
            out_specs=pl.BlockSpec(out_shape, lambda j, chan: (0, 0, 0, 0)),
            scratch_shapes=[
                pltpu.VMEM((spectra, ROWS, lanes), jnp.float32),
                pltpu.VMEM((part_rows, lanes), jnp.float32),
                pltpu.VMEM((frame_len, spectra * lanes), jnp.bfloat16),
                pltpu.VMEM((columns * spectra, lanes), jnp.float32),
            ],
        ),
        out_shape=jax.ShapeDtypeStruct(out_shape, jnp.bfloat16),
        compiler_params=pltpu.CompilerParams(
            dimension_semantics=("arbitrary",), vmem_limit_bytes=VMEM
        ),
        cost_estimate=pl.CostEstimate(
            flops=2 * (columns + FILTER_COST * taps) * frame_len * spectra * lanes,
            bytes_accessed=4 * n_frames * frame_len * lanes + 2 * columns * spectra * lanes,
            transcendentals=0,
        ),
    )(chan_map, samples, *halos, scales, weights, table)


def correlate_kernel(scale, *refs):
    cells_ref, *before, out_ref = refs
    times, bands, _, _, spectra, lanes = cells_ref.shape
    parts = [
        jnp.concatenate(
            [cells_ref[:, band, 0, part].reshape(times * spectra, lanes) for band in range(bands)], axis=1
        )
        for part in range(2)
    ]
    turned = [part.T for part in parts]
    dot = functools.partial(jnp.dot, preferred_element_type=jnp.float32)
    real = dot(turned[0], parts[0]) + dot(turned[1], parts[1])
    imag = dot(turned[1], parts[0]) - dot(turned[0], parts[1])
    both = real + imag
    if before:
        both = (both + before[0][0]) * (0.5 * scale)
        mirrored = both.T
        out_ref[0, 0] = both + mirrored
        out_ref[1, 0] = both - mirrored
    else:
        out_ref[0] = both


def correlate(cells, before, scale):
    times, bands, channels, _, spectra, lanes = cells.shape
    inputs = bands * lanes
    sums_spec = pl.BlockSpec((1, inputs, inputs), lambda c: (c, 0, 0))
    in_specs = [pl.BlockSpec((times, bands, 1, 2, spectra, lanes), lambda c: (0, 0, c, 0, 0, 0))]
    if before is None:
        more, out_shape, out_spec = [], (channels, inputs, inputs), sums_spec
    else:
        more, out_shape = [before], (2, channels, inputs, inputs)
        out_spec = pl.BlockSpec((2, 1, inputs, inputs), lambda c: (0, c, 0, 0))
        in_specs.append(sums_spec)
    return pl.pallas_call(
        functools.partial(correlate_kernel, scale),
        grid=(channels,),
        in_specs=in_specs,
        out_specs=out_spec,
        out_shape=jax.ShapeDtypeStruct(out_shape, jnp.float32),
        compiler_params=pltpu.CompilerParams(
            dimension_semantics=("arbitrary",), vmem_limit_bytes=VMEM
        ),
        cost_estimate=pl.CostEstimate(
            flops=8 * channels * inputs * inputs * times * spectra,
            bytes_accessed=2 * cells.size + 8 * channels * inputs * inputs,
            transcendentals=0,
        ),
    )(cells, *more)


def per_device(samples, input_gain, pfb_weights, chan_map):
    taps, frame_len = pfb_weights.shape
    row_count, lanes = samples.shape
    own = row_count // frame_len
    times = lax.axis_size("ta")
    bands = lax.axis_size("ba")
    dests = times * bands
    ahead = taps // 2
    behind = taps - 1 - ahead
    frames = samples.reshape(own, frame_len, lanes)

    head, tail = calibrate_ends(frames, input_gain[None, :], ahead, behind)
    history = lax.ppermute(tail, "ta", [(i, i + 1) for i in range(times - 1)])
    future = lax.ppermute(head, "ta", [(i, (i - 1) % times) for i in range(times)])
    is_last = lax.axis_index("ta") == times - 1
    scales = jnp.stack([input_gain, jnp.where(is_last, 0.0, input_gain)])
    table = build_table(chan_map.shape[0], frame_len)

    inner = [[(0, f, 0) for f in range(1, own)]]
    outer = [
        [(1, f, 0) for f in range(behind)] + [(0, f, 0) for f in range(taps)],
        [(0, f, 1) for f in range(own - taps + 1, own)] + [(2, f, 0) for f in range(ahead)],
    ]

    def turn(spectra):
        got = lax.all_to_all(spectra, ("ta", "ba"), 0, 0, tiled=True)
        _, columns, count, _ = got.shape
        return got.reshape(times, bands, columns // 2, 2, count, lanes)

    shared = (scales, pfb_weights, table)
    first = turn(transform(inner, taps, dests, chan_map, frames, [], *shared))
    second = turn(transform(outer, taps, dests, chan_map, frames, [history, future], *shared))
    sums = correlate(first, None, 1.0)
    return correlate(second, sums, 1.0 / (times * own))


def solution(mesh):
    placed = (P("ta", "ba"), P("ba"), P(), P())
    return jax.shard_map(
        per_device,
        mesh=mesh,
        in_specs=placed,
        out_specs=P(None, ("ta", "ba"), None, None),
        check_vma=False,
    )
```

time: 345 us -> 182 us (0.53)
  blocking collectives: 109 us -> 0 us
  Pallas kernels: 0 us -> 84.3 us
  other arithmetic: 75.7 us -> 0.54 us
  local copies, waits for them, and re-layouts: 48.1 us -> 1.37 us
  matrix products: 36 us -> 0 us
  starting transfers between devices: 3.23 us -> 27.2 us
  waiting for transfers between devices: 72 us -> 68.3 us
    all_to_all x1 -> x0, blocking collectives: 109 us -> none  [per_device(): lax.all_to_all(spectra.reshape(count, columns, spectra_dev, inputs_dev),...]
    pallas_call x0 -> x5, Pallas kernels: none -> 84.3 us  [the longest x2 60.4 us: transform(): pl.pallas_call(functools.partial(spectra_kernel, segments, taps), grid_sp...]
    ppermute x1 -> x2, waiting for transfers between devices: 72 us -> 5.98 us  [the longest x1 5.98 us: per_device(): lax.ppermute(head, 'ta', [(i, (i - 1) % times) for i in range(times)])]
    all_to_all x0 -> x2, waiting for transfers between devices: none -> 62.3 us  [turn(): got = lax.all_to_all(spectra, ('ta', 'ba'), 0, 0, tiled=True)]
    dot_general x1 -> x0, other arithmetic: 46.9 us -> none  [per_device(): jnp.einsum('kn,sni->ksi', dft_table, filtered, preferred_element_type=jnp...]
    reshape x3 -> x0, local copies, waits for them, and re-layouts: 38.2 us -> none  [the longest x1 16 us: per_device(): turned.reshape(times, bands, columns // 2, 2, spectra_dev, inputs_dev)]
    dot_general x3 -> x0, matrix products: 36 us -> none  [the longest x1 14.3 us: per_device(): jnp.einsum('kn,sni->ksi', dft_table, filtered, preferred_element_type=jnp...]
    all_to_all x0 -> x2, starting transfers between devices: none -> 23.2 us  [turn(): got = lax.all_to_all(spectra, ('ta', 'ba'), 0, 0, tiled=True)]
  transfers between devices with their start and end apart: 1 -> 4, of which waited for: 1 -> 3; matrix products, arithmetic and copies ran while one was open for 4% -> 0% of each run, Pallas kernels for 0% -> 38%
where the time goes in v2:
time: 182 us
  Pallas kernels  84.3 us (46%)
  waiting for transfers between devices  68.3 us (38%)
  starting transfers between devices  27.2 us (15%)
    all_to_all x2, waiting for transfers between devices, turn(): got = lax.all_to_all(spectra, ('ta', 'ba'), 0, 0, tiled=True)  62.3 us
    pallas_call x2, Pallas kernels, transform(): pl.pallas_call(functools.partial(spectra_kernel, segments, taps), grid_sp...  60.4 us
    all_to_all x2, starting transfers between devices, turn(): got = lax.all_to_all(spectra, ('ta', 'ba'), 0, 0, tiled=True)  23.2 us
    pallas_call x2, Pallas kernels, correlate(): pl.pallas_call(functools.partial(correlate_kernel, scale), grid=(channels...  18 us
    ppermute x1, waiting for transfers between devices, per_device(): lax.ppermute(head, 'ta', [(i, (i - 1) % times) for i in range(times)])  5.98 us
    pallas_call x1, Pallas kernels, calibrate_ends(): pl.pallas_call(functools.partial(calibrate_kernel, ahead, behind), grid=(...  5.94 us
  transfers between devices with their start and end apart: 4, of which 3 were waited for; matrix products, arithmetic and copies ran while one was open for 0% of the time, Pallas kernels for 38%

profile of v2, /device:TPU:4, one launch (start us, length us, event | category | flops | bytes accessed | tf_op | source)
XLA Modules:
  0.0 181.8 jit_solution(2619674962083595111)
XLA Ops:
  0.0 0.0 copy-start
  0.0 5.9 %shard_map.55 = (bf16[8,1024,128]{2,1,0:T(8,128)(2,1)}, bf16[7,1024,128]{2,1,0:T(8,128)(2,1)}) custom-call(s32[32,1024,128]{2,1,0:T(8,128)} %bitcast.6, s32[32,1024,128]{2,1,0:T(8,128)} %bitcast.7, f32[1,128]{1,0:T(1,128)} %bitcast.10), custom_call_target="tpu_custom_call" | custom-call | tf_op jit(solution)/shard_map/pallas_call | solution.py:38
  5.9 3.1 %collective-permute-start = (bf16[7,1024,128]{2,1,0:T(8,128)(2,1)}, bf16[7,1024,128]{2,1,0:T(8,128)(2,1)}, u32[]{:S(2)}, u32[]{:S(2)}) collective-permute-start(bf16[7,1024,128]{2,1,0:T(8,128)(2,1)} %get-tuple-element.7), channel_id=1, source_target_pairs={{0,4},{4,8},{8,12},{12,16},{16,20},{20,24},{24,28},{28,32},{32,36}... | collective-permute-start | bytes 5505032 | tf_op jit(solution)/shard_map/ppermute | solution.py:237
  9.0 0.9 collective-permute-start.1
  9.9 0.0 copy-done
  10.0 0.5 pad_maximum_fusion.refs_4_.refs_2_
  10.5 29.9 %shard_map.57 = bf16[128,8,16,128]{3,2,1,0:T(8,128)(2,1)} custom-call(s32[512]{0:T(512)} %refs_0_.3, s32[32,1024,128]{2,1,0:T(8,128)} %bitcast.8, f32[2,128]{1,0:T(2,128)} %pad_maximum_fusion.refs_4_.refs_2_, f32[16,1024]{1,0:T(8,128)} %refs_3_.1, bf16[1024,1024]{1,0:T(8,128)(2,1)} %constant.12.clone.refs_6_.refs_4_), custom_call_target="tpu_custom_call" | custom-call | flops 73014444032 | bytes 20971520 | tf_op jit(solution)/shard_map/pallas_call | solution.py:148
  40.4 11.5 %all-to-all-start.1 = ((bf16[128,8,16,128]{3,2,1,0:T(8,128)(2,1)}), bf16[128,8,16,128]{3,2,1,0:T(8,128)(2,1)}, u32[]{:S(2)}, u32[]{:S(2)}) async-start(bf16[128,8,16,128]{3,2,1,0:T(8,128)(2,1)} %shard_map.57), calls=%async_computation.1 | async-start | bytes 8388608 | tf_op jit(solution)/shard_map/all_to_all | solution.py:250
  51.9 0.0 collective-permute-done.refs_2_
  51.9 6.0 %collective-permute-done.1.refs_3_ = bf16[8,1024,128]{2,1,0:T(8,128)(2,1)S(1)} collective-permute-done((bf16[8,1024,128]{2,1,0:T(8,128)(2,1)}, bf16[8,1024,128]{2,1,0:T(8,128)(2,1)S(1)}, u32[]{:S(2)}, u32[]{:S(2)}) %collective-permute-start.1) | collective-permute-done | bytes 2097184 | tf_op jit(solution)/shard_map/ppermute | solution.py:238
  57.9 0.0 copy-start.1
  57.9 1.4 copy-done.1
  59.2 30.5 %shard_map.56 = bf16[128,8,16,128]{3,2,1,0:T(8,128)(2,1)} custom-call(s32[512]{0:T(512)} %refs_0_.3, s32[32,1024,128]{2,1,0:T(8,128)} %bitcast.9, bf16[7,1024,128]{2,1,0:T(8,128)(2,1)} %collective-permute-done.refs_2_, bf16[8,1024,128]{2,1,0:T(8,128)(2,1)} %copy-done.1, f32[2,128]{1,0:T(2,128)} %pad_maximum_fusion.refs_4_.refs_2_, f32[16,1024]{1,0:T(8,128)} %refs_3_.1, ...), custom_call_target="tpu_custom_call" | custom-call | flops 73014444032 | bytes 20971520 | tf_op jit(solution)/shard_map/pallas_call | solution.py:148
  89.8 17.5 %all-to-all-done.1 = bf16[128,8,16,128]{3,2,1,0:T(8,128)(2,1)} async-done(((bf16[128,8,16,128]{3,2,1,0:T(8,128)(2,1)}), bf16[128,8,16,128]{3,2,1,0:T(8,128)(2,1)}, u32[]{:S(2)}, u32[]{:S(2)}) %all-to-all-start.1) | async-done | bytes 4194336 | tf_op jit(solution)/shard_map/all_to_all | solution.py:250
  107.2 11.7 %all-to-all-start = ((bf16[128,8,16,128]{3,2,1,0:T(8,128)(2,1)}), bf16[128,8,16,128]{3,2,1,0:T(8,128)(2,1)}, u32[]{:S(2)}, u32[]{:S(2)}) async-start(bf16[128,8,16,128]{3,2,1,0:T(8,128)(2,1)} %shard_map.56), calls=%async_computation | async-start | bytes 8388608 | tf_op jit(solution)/shard_map/all_to_all | solution.py:250
  118.9 7.8 %shard_map.58.refs_1_ = f32[4,512,512]{2,1,0:T(8,128)} custom-call(bf16[32,4,4,2,16,128]{5,4,3,2,1,0:T(8,128)(2,1)} %bitcast.4.refs_0_), custom_call_target="tpu_custom_call" | custom-call | flops 4294967296 | bytes 12582912 | tf_op jit(solution)/shard_map/pallas_call | solution.py:208
  126.8 44.9 %all-to-all-done = bf16[128,8,16,128]{3,2,1,0:T(8,128)(2,1)} async-done(((bf16[128,8,16,128]{3,2,1,0:T(8,128)(2,1)}), bf16[128,8,16,128]{3,2,1,0:T(8,128)(2,1)}, u32[]{:S(2)}, u32[]{:S(2)}) %all-to-all-start) | async-done | bytes 4194336 | tf_op jit(solution)/shard_map/all_to_all | solution.py:250
  171.6 10.1 %shard_map.59 = f32[2,4,512,512]{3,2,1,0:T(8,128)} custom-call(bf16[32,4,4,2,16,128]{5,4,3,2,1,0:T(8,128)(2,1)} %bitcast.3.refs_0_, f32[4,512,512]{2,1,0:T(8,128)} %shard_map.58.refs_1_), custom_call_target="tpu_custom_call" | custom-call | flops 4294967296 | bytes 12582912 | tf_op jit(solution)/shard_map/pallas_call | solution.py:208
  (1 shorter events, 0.0 us)
Async XLA Ops:
  0.0 9.9 %copy-start = (f32[128]{0:T(128)S(1)}, f32[128]{0:T(128)}, u32[]{:S(2)}) copy-start(f32[128]{0:T(128)} %param.6) | copy-start | bytes 1540
  5.9 45.9 %collective-permute-start = (bf16[7,1024,128]{2,1,0:T(8,128)(2,1)}, bf16[7,1024,128]{2,1,0:T(8,128)(2,1)}, u32[]{:S(2)}, u32[]{:S(2)}) collective-permute-start(bf16[7,1024,128]{2,1,0:T(8,128)(2,1)} %get-tuple-element.7), channel_id=1, source_target_pairs={{0,4},{4,8},{8,12},{12,16},{16,20},{20,24},{24,28},{28,32},{32,36}... | collective-permute-start | bytes 5505032 | tf_op jit(solution)/shard_map/ppermute | solution.py:237
  9.0 48.8 %collective-permute-start.1 = (bf16[8,1024,128]{2,1,0:T(8,128)(2,1)}, bf16[8,1024,128]{2,1,0:T(8,128)(2,1)S(1)}, u32[]{:S(2)}, u32[]{:S(2)}) collective-permute-start(bf16[8,1024,128]{2,1,0:T(8,128)(2,1)} %get-tuple-element.8), channel_id=1, source_target_pairs={{0,124},{4,0},{8,4},{12,8},{16,12},{20,16},{24,20},{28,24},{32,28}... | collective-permute-start | bytes 6291464 | tf_op jit(solution)/shard_map/ppermute | solution.py:238
  40.4 66.9 %all-to-all-start.1 = ((bf16[128,8,16,128]{3,2,1,0:T(8,128)(2,1)}), bf16[128,8,16,128]{3,2,1,0:T(8,128)(2,1)}, u32[]{:S(2)}, u32[]{:S(2)}) async-start(bf16[128,8,16,128]{3,2,1,0:T(8,128)(2,1)} %shard_map.57), calls=%async_computation.1 | async-start | bytes 8388608 | tf_op jit(solution)/shard_map/all_to_all | solution.py:250
  57.9 1.4 copy-start.1
  107.2 64.4 %all-to-all-start = ((bf16[128,8,16,128]{3,2,1,0:T(8,128)(2,1)}), bf16[128,8,16,128]{3,2,1,0:T(8,128)(2,1)}, u32[]{:S(2)}, u32[]{:S(2)}) async-start(bf16[128,8,16,128]{3,2,1,0:T(8,128)(2,1)} %shard_map.56), calls=%async_computation | async-start | bytes 8388608 | tf_op jit(solution)/shard_map/all_to_all | solution.py:250

commit v3 on v2

v3 whole, which is shorter than its diff:
```python
import functools
import math

import jax
import jax.numpy as jnp
import numpy as np
from jax import lax
from jax.experimental import pallas as pl
from jax.experimental.pallas import tpu as pltpu
from jax.sharding import PartitionSpec as P

LANES = 128
ROWS = 16
STEPS = 8
CALIBRATE_STEPS = 2
VMEM = 60 * 1024 * 1024
FILTER_COST = 1024


def build_table(channels, frame_len):
    turns = np.arange(channels)[:, None] * np.arange(frame_len)[None, :] % frame_len
    angle = turns * (2.0 * np.pi / frame_len)
    both = np.stack([np.cos(angle), -np.sin(angle)], axis=1) / math.sqrt(frame_len)
    return jnp.asarray(both.reshape(2 * channels, frame_len), dtype=jnp.bfloat16)


def calibrate_kernel(frames_ref, gain_ref, out_ref):
    values = frames_ref[...].astype(jnp.float32)
    out_ref[...] = (values * gain_ref[...][None]).astype(jnp.bfloat16)


def calibrate(frames, gain, place, count):
    _, frame_len, lanes = frames.shape
    part = frame_len // CALIBRATE_STEPS
    return pl.pallas_call(
        calibrate_kernel,
        grid=(CALIBRATE_STEPS,),
        in_specs=[
            pl.BlockSpec((count, part, lanes), lambda j: (place, j, 0)),
            pl.BlockSpec((1, lanes), lambda j: (0, 0)),
        ],
        out_specs=pl.BlockSpec((count, part, lanes), lambda j: (0, j, 0)),
        out_shape=jax.ShapeDtypeStruct((count, frame_len, lanes), jnp.bfloat16),
        compiler_params=pltpu.CompilerParams(
            dimension_semantics=("arbitrary",), vmem_limit_bytes=VMEM
        ),
    )(frames, gain)


def filter_rows(segments, taps, row, samples_ref, halo_refs, scale_ref, weights, before, emit):
    both = pl.ds(row, ROWS)
    for half in range(2):
        rows = pl.ds(row + half * 8, 8)
        weight = [jnp.broadcast_to(weights[rows, t : t + 1], (8, LANES)) for t in range(taps)]
        base = 0
        for segment in segments:
            count = len(segment) - taps + 1
            sums = {s: before(base + s, rows) for s in range(count)} if before else {}
            for place, entry in enumerate(segment):
                if entry is not None:
                    source, frame, scale_row = entry
                    if source == 0:
                        raw = samples_ref[frame, rows, :].astype(jnp.float32)
                        value = raw * scale_ref[scale_row : scale_row + 1, :]
                        value = value.astype(jnp.bfloat16).astype(jnp.float32)
                    else:
                        value = halo_refs[source - 1][frame, both, :].astype(jnp.float32)
                        value = value[half * 8 : half * 8 + 8]
                    for s in range(max(0, place - taps + 1), min(count, place + 1)):
                        term = value * weight[place - s]
                        sums[s] = sums[s] + term if s in sums else term
                done = place - taps + 1
                if done >= 0:
                    emit(base + done, half, sums.pop(done))
            base += count


def partial_kernel(segments, taps, samples_ref, halo_ref, scale_ref, weight_ref, out_ref, weights):
    weights[:, :taps] = weight_ref[...].T

    def tile(index, carry):
        row = pl.multiple_of(index * ROWS, ROWS)

        def emit(s, half, total):
            out_ref[s, pl.ds(row + half * 8, 8), :] = total

        filter_rows(
            segments, taps, row, samples_ref, [halo_ref], scale_ref, weights, None, emit
        )
        return carry

    lax.fori_loop(0, out_ref.shape[1] // ROWS, tile, 0)


def filter_part(segments, taps, samples, halo, scales, weights):
    n_frames, frame_len, lanes = samples.shape
    spectra = sum(len(segment) - taps + 1 for segment in segments)
    part_rows = frame_len // STEPS
    index = lambda j: (0, j, 0)
    return pl.pallas_call(
        functools.partial(partial_kernel, segments, taps),
        grid=(STEPS,),
        in_specs=[
            pl.BlockSpec((n_frames, part_rows, lanes), index),
            pl.BlockSpec((halo.shape[0], part_rows, lanes), index),
            pl.BlockSpec(scales.shape, lambda j: (0, 0)),
            pl.BlockSpec((taps, part_rows), lambda j: (0, j)),
        ],
        out_specs=pl.BlockSpec((spectra, part_rows, lanes), index),
        out_shape=jax.ShapeDtypeStruct((spectra, frame_len, lanes), jnp.float32),
        scratch_shapes=[pltpu.VMEM((part_rows, lanes), jnp.float32)],
        compiler_params=pltpu.CompilerParams(
            dimension_semantics=("arbitrary",), vmem_limit_bytes=VMEM
        ),
        cost_estimate=pl.CostEstimate(
            flops=2 * FILTER_COST * taps * frame_len * spectra * lanes,
            bytes_accessed=4 * (n_frames + spectra) * frame_len * lanes,
            transcendentals=0,
        ),
    )(samples, halo, scales, weights)


def spectra_kernel(segments, taps, chan_ref, source_ref, *refs):
    *halo_refs, scale_ref, weight_ref, table, out_ref, weights, filtered, turned = refs
    step = pl.program_id(0)
    spectra = sum(len(segment) - taps + 1 for segment in segments)
    part_rows = source_ref.shape[1]
    columns = table.shape[0]
    pairs = spectra // 2

    @pl.when(step < STEPS)
    def _():
        weights[:, :taps] = weight_ref[...].T

        def tile(index, carry):
            row = pl.multiple_of(index * ROWS, ROWS)
            start = pl.multiple_of(step * part_rows + row, ROWS)

            def emit(s, half, total):
                filtered[pl.ds(start + half * 8, 8), s * LANES : (s + 1) * LANES] = total

            before = (lambda s, rows: source_ref[s, rows, :]) if halo_refs else None
            filter_rows(
                segments, taps, row, source_ref, halo_refs, scale_ref, weights, before, emit
            )
            return carry

        lax.fori_loop(0, part_rows // ROWS, tile, 0)

    @pl.when(step >= STEPS)
    def _():
        pair = step - STEPS
        rhs = filtered[:, pl.ds(pl.multiple_of(pair * 2 * LANES, 2 * LANES), 2 * LANES)]
        rhs = rhs.astype(jnp.bfloat16)
        block = 256
        for c in range(0, columns, block):
            product = jnp.dot(table[c : c + block, :], rhs, preferred_element_type=jnp.float32)
            for odd in range(2):
                turned[pl.ds(c * spectra + pair * 2 + odd, block, stride=spectra), :] = product[
                    :, odd * LANES : (odd + 1) * LANES
                ]

    @pl.when(step == STEPS + pairs - 1)
    def _():
        slots = out_ref.shape[1] // 2
        group = 2

        def emit(index, carry):
            rows = 2 * spectra
            places = [(index * group + here, slot) for here in range(group) for slot in range(slots)]
            values = []
            for dest, slot in places:
                first = chan_ref[dest * slots + slot] * rows
                values.append(turned[pl.ds(pl.multiple_of(first, rows), rows), :].astype(jnp.bfloat16))
            for (dest, slot), value in zip(places, values):
                out_ref[dest, 2 * slot : 2 * slot + 2] = value.reshape(2, spectra, LANES)
            return carry

        lax.fori_loop(0, out_ref.shape[0] // group, emit, 0)


def transform(segments, taps, dests, chan_map, source, halos, scales, weights, table):
    n_frames, frame_len, lanes = source.shape
    columns = table.shape[0]
    spectra = sum(len(segment) - taps + 1 for segment in segments)
    part_rows = frame_len // STEPS
    steps = STEPS + spectra // 2
    index = lambda j, chan: (0, jnp.minimum(j, STEPS - 1), 0)
    in_specs = [pl.BlockSpec((n_frames, part_rows, lanes), index)]
    in_specs += [pl.BlockSpec((halo.shape[0], part_rows, lanes), index) for halo in halos]
    in_specs += [
        pl.BlockSpec(scales.shape, lambda j, chan: (0, 0)),
        pl.BlockSpec((taps, part_rows), lambda j, chan: (0, jnp.minimum(j, STEPS - 1))),
        pl.BlockSpec(table.shape, lambda j, chan: (0, 0)),
    ]
    out_shape = (dests, 2 * chan_map.shape[0] // dests, spectra, lanes)
    return pl.pallas_call(
        functools.partial(spectra_kernel, segments, taps),
        grid_spec=pltpu.PrefetchScalarGridSpec(
            num_scalar_prefetch=1,
            grid=(steps,),
            in_specs=in_specs,
            out_specs=pl.BlockSpec(out_shape, lambda j, chan: (0, 0, 0, 0)),
            scratch_shapes=[
                pltpu.VMEM((part_rows, lanes), jnp.float32),
                pltpu.VMEM((frame_len, spectra * lanes), jnp.float32),
                pltpu.VMEM((columns * spectra, lanes), jnp.float32),
            ],
        ),
        out_shape=jax.ShapeDtypeStruct(out_shape, jnp.bfloat16),
        compiler_params=pltpu.CompilerParams(
            dimension_semantics=("arbitrary",), vmem_limit_bytes=VMEM
        ),
        cost_estimate=pl.CostEstimate(
            flops=2 * (columns + (0 if halos else FILTER_COST * taps)) * frame_len * spectra * lanes,
            bytes_accessed=4 * n_frames * frame_len * lanes + 2 * columns * spectra * lanes,
            transcendentals=0,
        ),
    )(chan_map, source, *halos, scales, weights, table)


def correlate_kernel(scale, *refs):
    cells_ref, *before, out_ref = refs
    times, bands, _, _, spectra, lanes = cells_ref.shape
    parts = [
        jnp.concatenate(
            [cells_ref[:, band, 0, part].reshape(times * spectra, lanes) for band in range(bands)], axis=1
        )
        for part in range(2)
    ]
    turned = [part.T for part in parts]
    dot = functools.partial(jnp.dot, preferred_element_type=jnp.float32)
    real = dot(turned[0], parts[0]) + dot(turned[1], parts[1])
    imag = dot(turned[1], parts[0]) - dot(turned[0], parts[1])
    both = real + imag
    if before:
        both = (both + before[0][0]) * (0.5 * scale)
        mirrored = both.T
        out_ref[0, 0] = both + mirrored
        out_ref[1, 0] = both - mirrored
    else:
        out_ref[0] = both


def correlate(cells, before, scale):
    times, bands, channels, _, spectra, lanes = cells.shape
    inputs = bands * lanes
    sums_spec = pl.BlockSpec((1, inputs, inputs), lambda c: (c, 0, 0))
    in_specs = [pl.BlockSpec((times, bands, 1, 2, spectra, lanes), lambda c: (0, 0, c, 0, 0, 0))]
    if before is None:
        more, out_shape, out_spec = [], (channels, inputs, inputs), sums_spec
    else:
        more, out_shape = [before], (2, channels, inputs, inputs)
        out_spec = pl.BlockSpec((2, 1, inputs, inputs), lambda c: (0, c, 0, 0))
        in_specs.append(sums_spec)
    return pl.pallas_call(
        functools.partial(correlate_kernel, scale),
        grid=(channels,),
        in_specs=in_specs,
        out_specs=out_spec,
        out_shape=jax.ShapeDtypeStruct(out_shape, jnp.float32),
        compiler_params=pltpu.CompilerParams(
            dimension_semantics=("arbitrary",), vmem_limit_bytes=VMEM
        ),
        cost_estimate=pl.CostEstimate(
            flops=8 * channels * inputs * inputs * times * spectra,
            bytes_accessed=2 * cells.size + 8 * channels * inputs * inputs,
            transcendentals=0,
        ),
    )(cells, *more)


def per_device(samples, input_gain, pfb_weights, chan_map):
    taps, frame_len = pfb_weights.shape
    row_count, lanes = samples.shape
    own = row_count // frame_len
    times = lax.axis_size("ta")
    bands = lax.axis_size("ba")
    dests = times * bands
    behind = taps // 2
    ahead = taps - 1 - behind
    frames = samples.reshape(own, frame_len, lanes)

    gain = input_gain[None, :]
    head = calibrate(frames, gain, 0, ahead)
    tail = calibrate(frames, gain, own // behind - 1, behind)
    future = lax.ppermute(head, "ta", [(i, (i - 1) % times) for i in range(times)])
    history = lax.ppermute(tail, "ta", [(i, i + 1) for i in range(times - 1)])
    is_last = lax.axis_index("ta") == times - 1
    scales = jnp.stack([input_gain, jnp.where(is_last, 0.0, input_gain)])
    table = build_table(chan_map.shape[0], frame_len)

    inner = [[(0, f, 0) for f in range(1, own)]]
    early = [
        [(1, f, 0) for f in range(behind)] + [(0, f, 0) for f in range(taps)],
        [(0, f, 1) for f in range(own - taps + 1, own)] + [None] * ahead,
    ]
    late = [[None] * (behind + taps), [None] * (taps - 1) + [(1, f, 0) for f in range(ahead)]]

    def turn(spectra):
        got = lax.all_to_all(spectra, ("ta", "ba"), 0, 0, tiled=True)
        _, columns, count, _ = got.shape
        return got.reshape(times, bands, columns // 2, 2, count, lanes)

    shared = (scales, pfb_weights, table)
    first = turn(transform(inner, taps, dests, chan_map, frames, [], *shared))
    part = filter_part(early, taps, frames, history, scales, pfb_weights)
    second = turn(transform(late, taps, dests, chan_map, part, [future], *shared))
    sums = correlate(first, None, 1.0)
    return correlate(second, sums, 1.0 / (times * own))


def solution(mesh):
    placed = (P("ta", "ba"), P("ba"), P(), P())
    return jax.shard_map(
        per_device,
        mesh=mesh,
        in_specs=placed,
        out_specs=P(None, ("ta", "ba"), None, None),
        check_vma=False,
    )
```

time: 182 us -> 177 us (0.973)
  waiting for transfers between devices: 68.3 us -> 56.3 us
  Pallas kernels: 84.3 us -> 93.8 us
  starting transfers between devices: 27.2 us -> 24.2 us
    pallas_call x1 -> x3, Pallas kernels: 5.94 us -> 24.3 us  [the longest x1 17.7 us: filter_part(): pl.pallas_call(functools.partial(partial_kernel, segments, taps), grid=(S...]
    pallas_call x2, Pallas kernels: 60.4 us -> 51.6 us  [transform(): pl.pallas_call(functools.partial(spectra_kernel, segments, taps), grid_sp...]
    all_to_all x2, waiting for transfers between devices: 62.3 us -> 54 us  [turn(): got = lax.all_to_all(spectra, ('ta', 'ba'), 0, 0, tiled=True)]
    ppermute x1, waiting for transfers between devices: 5.98 us -> 0.01 us  [per_device(): lax.ppermute(head, 'ta', [(i, (i - 1) % times) for i in range(times)])]
    all_to_all x2, starting transfers between devices: 23.2 us -> 20.2 us  [turn(): got = lax.all_to_all(spectra, ('ta', 'ba'), 0, 0, tiled=True)]
    ppermute x1, waiting for transfers between devices: 0.01 us -> 2.34 us  [per_device(): history = lax.ppermute(tail, 'ta', [(i, i + 1) for i in range(times - 1)])]
  transfers between devices with their start and end apart: 4 -> 4, of which waited for: 3 -> 3; matrix products, arithmetic and copies ran while one was open for 0% -> 0% of each run, Pallas kernels for 38% -> 46%
where the time goes in v3:
time: 177 us; the launch traced here: 176 us
  Pallas kernels  93.8 us (53%)
  waiting for transfers between devices  56.3 us (32%)
  starting transfers between devices  24.2 us (14%)
    all_to_all x2, waiting for transfers between devices, turn(): got = lax.all_to_all(spectra, ('ta', 'ba'), 0, 0, tiled=True)  54 us
    pallas_call x2, Pallas kernels, transform(): pl.pallas_call(functools.partial(spectra_kernel, segments, taps), grid_sp...  51.6 us
    all_to_all x2, starting transfers between devices, turn(): got = lax.all_to_all(spectra, ('ta', 'ba'), 0, 0, tiled=True)  20.2 us
    pallas_call x2, Pallas kernels, correlate(): pl.pallas_call(functools.partial(correlate_kernel, scale), grid=(channels...  18 us
    pallas_call x1, Pallas kernels, filter_part(): pl.pallas_call(functools.partial(partial_kernel, segments, taps), grid=(S...  17.7 us
    pallas_call x2, Pallas kernels, calibrate(): pl.pallas_call(calibrate_kernel, grid=(CALIBRATE_STEPS,), in_specs=[pl.Bl...  6.55 us
  transfers between devices with their start and end apart: 4, of which 3 were waited for; matrix products, arithmetic and copies ran while one was open for 0% of the time, Pallas kernels for 46%

profile of v3, /device:TPU:4, one launch (start us, length us, event | category | flops | bytes accessed | tf_op | source)
XLA Modules:
  0.0 176.3 jit_solution(1503635269284624330)
XLA Ops:
  0.0 3.4 %shard_map.55 = bf16[8,1024,128]{2,1,0:T(8,128)(2,1)} custom-call(s32[32,1024,128]{2,1,0:T(8,128)} %bitcast.6, f32[1,128]{1,0:T(1,128)} %bitcast.10), custom_call_target="tpu_custom_call" | custom-call | tf_op jit(solution)/shard_map/pallas_call | solution.py:35
  3.4 0.0 copy-start.1
  3.4 3.2 %collective-permute-start = (bf16[8,1024,128]{2,1,0:T(8,128)(2,1)}, bf16[8,1024,128]{2,1,0:T(8,128)(2,1)}, u32[]{:S(2)}, u32[]{:S(2)}) collective-permute-start(bf16[8,1024,128]{2,1,0:T(8,128)(2,1)} %shard_map.55), channel_id=1, source_target_pairs={{0,4},{4,8},{8,12},{12,16},{16,20},{20,24},{24,28},{28,32},{32,36}... | collective-permute-start | bytes 6291464 | tf_op jit(solution)/shard_map/ppermute | solution.py:288
  6.6 3.2 %shard_map.57 = bf16[7,1024,128]{2,1,0:T(8,128)(2,1)} custom-call(s32[32,1024,128]{2,1,0:T(8,128)} %bitcast.7, f32[1,128]{1,0:T(1,128)} %bitcast.11), custom_call_target="tpu_custom_call" | custom-call | tf_op jit(solution)/shard_map/pallas_call | solution.py:35
  9.8 0.8 collective-permute-start.1
  10.6 0.0 copy-done.1
  10.6 0.6 pad_maximum_fusion.scale_ref.refs_1_.refs_0_
  11.2 29.3 %shard_map.59 = bf16[128,8,16,128]{3,2,1,0:T(8,128)(2,1)} custom-call(s32[512]{0:T(512)} %chan_ref.3, s32[32,1024,128]{2,1,0:T(8,128)} %bitcast.8, f32[2,128]{1,0:T(2,128)} %pad_maximum_fusion.scale_ref.refs_1_.refs_0_, f32[16,1024]{1,0:T(8,128)} %refs_1_.1, bf16[1024,1024]{1,0:T(8,128)(2,1)} %constant.12.clone.refs_3_.refs_2_), custom_call_target="tpu_custom_call" | custom-call | flops 73014444032 | bytes 20971520 | tf_op jit(solution)/shard_map/pallas_call | solution.py:197
  40.5 11.5 %all-to-all-start.1 = ((bf16[128,8,16,128]{3,2,1,0:T(8,128)(2,1)}), bf16[128,8,16,128]{3,2,1,0:T(8,128)(2,1)}, u32[]{:S(2)}, u32[]{:S(2)}) async-start(bf16[128,8,16,128]{3,2,1,0:T(8,128)(2,1)} %shard_map.59), calls=%async_computation.1 | async-start | bytes 8388608 | tf_op jit(solution)/shard_map/all_to_all | solution.py:301
  52.0 2.3 %collective-permute-done.halo_ref = bf16[8,1024,128]{2,1,0:T(8,128)(2,1)} collective-permute-done((bf16[8,1024,128]{2,1,0:T(8,128)(2,1)}, bf16[8,1024,128]{2,1,0:T(8,128)(2,1)}, u32[]{:S(2)}, u32[]{:S(2)}) %collective-permute-start) | collective-permute-done | bytes 2097184 | tf_op jit(solution)/shard_map/ppermute | solution.py:288
  54.3 17.7 %shard_map.56.source_ref = f32[16,1024,128]{2,1,0:T(8,128)} custom-call(s32[32,1024,128]{2,1,0:T(8,128)} %bitcast.9, bf16[8,1024,128]{2,1,0:T(8,128)(2,1)} %collective-permute-done.halo_ref, f32[2,128]{1,0:T(2,128)} %pad_maximum_fusion.scale_ref.refs_1_.refs_0_, f32[16,1024]{1,0:T(8,128)} %refs_1_.1), custom_call_target="tpu_custom_call" | custom-call | flops 68719476736 | bytes 25165824 | tf_op jit(solution)/shard_map/pallas_call | solution.py:100
  72.1 0.0 collective-permute-done.1.refs_0_
  72.1 0.0 copy-start
  72.1 1.3 copy-done
  73.3 22.3 %shard_map.58 = bf16[128,8,16,128]{3,2,1,0:T(8,128)(2,1)} custom-call(s32[512]{0:T(512)} %chan_ref.3, f32[16,1024,128]{2,1,0:T(8,128)} %shard_map.56.source_ref, bf16[7,1024,128]{2,1,0:T(8,128)(2,1)} %copy-done, f32[2,128]{1,0:T(2,128)} %pad_maximum_fusion.scale_ref.refs_1_.refs_0_, f32[16,1024]{1,0:T(8,128)} %refs_1_.1, ...), custom_call_target="tpu_custom_call" | custom-call | flops 4294967296 | bytes 12582912 | tf_op jit(solution)/shard_map/pallas_call | solution.py:197
  95.6 9.1 %all-to-all-done.1 = bf16[128,8,16,128]{3,2,1,0:T(8,128)(2,1)} async-done(((bf16[128,8,16,128]{3,2,1,0:T(8,128)(2,1)}), bf16[128,8,16,128]{3,2,1,0:T(8,128)(2,1)}, u32[]{:S(2)}, u32[]{:S(2)}) %all-to-all-start.1) | async-done | bytes 4194336 | tf_op jit(solution)/shard_map/all_to_all | solution.py:301
  104.8 8.7 %all-to-all-start = ((bf16[128,8,16,128]{3,2,1,0:T(8,128)(2,1)}), bf16[128,8,16,128]{3,2,1,0:T(8,128)(2,1)}, u32[]{:S(2)}, u32[]{:S(2)}) async-start(bf16[128,8,16,128]{3,2,1,0:T(8,128)(2,1)} %shard_map.58), calls=%async_computation | async-start | bytes 8388608 | tf_op jit(solution)/shard_map/all_to_all | solution.py:301
  113.4 7.8 %shard_map.60.refs_1_ = f32[4,512,512]{2,1,0:T(8,128)} custom-call(bf16[32,4,4,2,16,128]{5,4,3,2,1,0:T(8,128)(2,1)} %bitcast.4.refs_0_), custom_call_target="tpu_custom_call" | custom-call | flops 4294967296 | bytes 12582912 | tf_op jit(solution)/shard_map/pallas_call | solution.py:256
  121.3 44.9 %all-to-all-done = bf16[128,8,16,128]{3,2,1,0:T(8,128)(2,1)} async-done(((bf16[128,8,16,128]{3,2,1,0:T(8,128)(2,1)}), bf16[128,8,16,128]{3,2,1,0:T(8,128)(2,1)}, u32[]{:S(2)}, u32[]{:S(2)}) %all-to-all-start) | async-done | bytes 4194336 | tf_op jit(solution)/shard_map/all_to_all | solution.py:301
  166.2 10.1 %shard_map.61 = f32[2,4,512,512]{3,2,1,0:T(8,128)} custom-call(bf16[32,4,4,2,16,128]{5,4,3,2,1,0:T(8,128)(2,1)} %bitcast.3.refs_0_, f32[4,512,512]{2,1,0:T(8,128)} %shard_map.60.refs_1_), custom_call_target="tpu_custom_call" | custom-call | flops 4294967296 | bytes 12582912 | tf_op jit(solution)/shard_map/pallas_call | solution.py:256
  (1 shorter events, 0.0 us)
Async XLA Ops:
  3.4 7.2 %copy-start.1 = (f32[128]{0:T(128)S(1)}, f32[128]{0:T(128)}, u32[]{:S(2)}) copy-start(f32[128]{0:T(128)} %param.6) | copy-start | bytes 1540
  3.4 51.0 %collective-permute-start = (bf16[8,1024,128]{2,1,0:T(8,128)(2,1)}, bf16[8,1024,128]{2,1,0:T(8,128)(2,1)}, u32[]{:S(2)}, u32[]{:S(2)}) collective-permute-start(bf16[8,1024,128]{2,1,0:T(8,128)(2,1)} %shard_map.55), channel_id=1, source_target_pairs={{0,4},{4,8},{8,12},{12,16},{16,20},{20,24},{24,28},{28,32},{32,36}... | collective-permute-start | bytes 6291464 | tf_op jit(solution)/shard_map/ppermute | solution.py:288
  9.8 62.3 %collective-permute-start.1 = (bf16[7,1024,128]{2,1,0:T(8,128)(2,1)}, bf16[7,1024,128]{2,1,0:T(8,128)(2,1)S(1)}, u32[]{:S(2)}, u32[]{:S(2)}) collective-permute-start(bf16[7,1024,128]{2,1,0:T(8,128)(2,1)} %shard_map.57), channel_id=1, source_target_pairs={{0,124},{4,0},{8,4},{12,8},{16,12},{20,16},{24,20},{28,24},{32,28}... | collective-permute-start | bytes 5505032 | tf_op jit(solution)/shard_map/ppermute | solution.py:287
  40.5 64.3 %all-to-all-start.1 = ((bf16[128,8,16,128]{3,2,1,0:T(8,128)(2,1)}), bf16[128,8,16,128]{3,2,1,0:T(8,128)(2,1)}, u32[]{:S(2)}, u32[]{:S(2)}) async-start(bf16[128,8,16,128]{3,2,1,0:T(8,128)(2,1)} %shard_map.59), calls=%async_computation.1 | async-start | bytes 8388608 | tf_op jit(solution)/shard_map/all_to_all | solution.py:301
  72.1 1.3 copy-start
  104.8 61.4 %all-to-all-start = ((bf16[128,8,16,128]{3,2,1,0:T(8,128)(2,1)}), bf16[128,8,16,128]{3,2,1,0:T(8,128)(2,1)}, u32[]{:S(2)}, u32[]{:S(2)}) async-start(bf16[128,8,16,128]{3,2,1,0:T(8,128)(2,1)} %shard_map.58), calls=%async_computation | async-start | bytes 8388608 | tf_op jit(solution)/shard_map/all_to_all | solution.py:301

commit v4 on v3

--- a/solution.py
+++ b/solution.py
@@ -219,55 +219,88 @@
     )(chan_map, source, *halos, scales, weights, table)
 
 
-def correlate_kernel(scale, *refs):
-    cells_ref, *before, out_ref = refs
-    times, bands, _, _, spectra, lanes = cells_ref.shape
+def sums_of(cells):
+    times, bands, _, spectra, lanes = cells.shape
     parts = [
         jnp.concatenate(
-            [cells_ref[:, band, 0, part].reshape(times * spectra, lanes) for band in range(bands)], axis=1
+            [cells[:, band, part].reshape(times * spectra, lanes) for band in range(bands)], axis=1
         )
         for part in range(2)
     ]
     turned = [part.T for part in parts]
     dot = functools.partial(jnp.dot, preferred_element_type=jnp.float32)
     real = dot(turned[0], parts[0]) + dot(turned[1], parts[1])
-    imag = dot(turned[1], parts[0]) - dot(turned[0], parts[1])
-    both = real + imag
-    if before:
-        both = (both + before[0][0]) * (0.5 * scale)
+    return real + (dot(turned[1], parts[0]) - dot(turned[0], parts[1]))
+
+
+def sums_kernel(cells_ref, out_ref):
+    out_ref[0] = sums_of(cells_ref.at[:, :, 0])
+
+
+def correlate_kernel(scale, cells_hbm, before_hbm, out_hbm, cells, before, out, cells_sem, before_sem, out_sem):
+    channels = cells.shape[0]
+    reads = [
+        (
+            pltpu.make_async_copy(cells_hbm.at[:, :, c], cells.at[c], cells_sem.at[c]),
+            pltpu.make_async_copy(before_hbm.at[c], before.at[c], before_sem.at[c]),
+        )
+        for c in range(channels)
+    ]
+    for read_cells, read_before in reads:
+        read_cells.start()
+        read_before.start()
+    writes = []
+    for c, (read_cells, read_before) in enumerate(reads):
+        read_cells.wait()
+        both = sums_of(cells.at[c])
+        read_before.wait()
+        both = (both + before[c]) * (0.5 * scale)
         mirrored = both.T
-        out_ref[0, 0] = both + mirrored
-        out_ref[1, 0] = both - mirrored
-    else:
-        out_ref[0] = both
+        out[c, 0] = both + mirrored
+        out[c, 1] = both - mirrored
+        writes.append(pltpu.make_async_copy(out.at[c], out_hbm.at[:, c], out_sem.at[c]))
+        writes[-1].start()
+    for write in writes:
+        write.wait()
 
 
 def correlate(cells, before, scale):
     times, bands, channels, _, spectra, lanes = cells.shape
     inputs = bands * lanes
-    sums_spec = pl.BlockSpec((1, inputs, inputs), lambda c: (c, 0, 0))
-    in_specs = [pl.BlockSpec((times, bands, 1, 2, spectra, lanes), lambda c: (0, 0, c, 0, 0, 0))]
+    params = dict(vmem_limit_bytes=VMEM)
+    cost = pl.CostEstimate(
+        flops=8 * channels * inputs * inputs * times * spectra,
+        bytes_accessed=2 * cells.size + 8 * channels * inputs * inputs,
+        transcendentals=0,
+    )
     if before is None:
-        more, out_shape, out_spec = [], (channels, inputs, inputs), sums_spec
-    else:
-        more, out_shape = [before], (2, channels, inputs, inputs)
-        out_spec = pl.BlockSpec((2, 1, inputs, inputs), lambda c: (0, c, 0, 0))
-        in_specs.append(sums_spec)
+        return pl.pallas_call(
+            sums_kernel,
+            grid=(channels,),
+            in_specs=[
+                pl.BlockSpec((times, bands, 1, 2, spectra, lanes), lambda c: (0, 0, c, 0, 0, 0))
+            ],
+            out_specs=pl.BlockSpec((1, inputs, inputs), lambda c: (c, 0, 0)),
+            out_shape=jax.ShapeDtypeStruct((channels, inputs, inputs), jnp.float32),
+            compiler_params=pltpu.CompilerParams(dimension_semantics=("arbitrary",), **params),
+            cost_estimate=cost,
+        )(cells)
     return pl.pallas_call(
         functools.partial(correlate_kernel, scale),
-        grid=(channels,),
-        in_specs=in_specs,
-        out_specs=out_spec,
-        out_shape=jax.ShapeDtypeStruct(out_shape, jnp.float32),
-        compiler_params=pltpu.CompilerParams(
-            dimension_semantics=("arbitrary",), vmem_limit_bytes=VMEM
-        ),
-        cost_estimate=pl.CostEstimate(
-            flops=8 * channels * inputs * inputs * times * spectra,
-            bytes_accessed=2 * cells.size + 8 * channels * inputs * inputs,
-            transcendentals=0,
-        ),
-    )(cells, *more)
+        in_specs=[pl.BlockSpec(memory_space=pl.ANY)] * 2,
+        out_specs=pl.BlockSpec(memory_space=pl.ANY),
+        out_shape=jax.ShapeDtypeStruct((2, channels, inputs, inputs), jnp.float32),
+        scratch_shapes=[
+            pltpu.VMEM((channels, times, bands, 2, spectra, lanes), cells.dtype),
+            pltpu.VMEM((channels, inputs, inputs), jnp.float32),
+            pltpu.VMEM((channels, 2, inputs, inputs), jnp.float32),
+            pltpu.SemaphoreType.DMA((channels,)),
+            pltpu.SemaphoreType.DMA((channels,)),
+            pltpu.SemaphoreType.DMA((channels,)),
+        ],
+        compiler_params=pltpu.CompilerParams(**params),
+        cost_estimate=cost,
+    )(cells, before)
 
 
 def per_device(samples, input_gain, pfb_weights, chan_map):

time: 177 us -> 176 us (level)
  no operation moved by 1% of the time
where the time goes in v4:
time: 176 us
  Pallas kernels  93.1 us (53%)
  waiting for transfers between devices  56.3 us (32%)
  starting transfers between devices  24.2 us (14%)
    all_to_all x2, waiting for transfers between devices, turn(): got = lax.all_to_all(spectra, ('ta', 'ba'), 0, 0, tiled=True)  54 us
    pallas_call x2, Pallas kernels, transform(): pl.pallas_call(functools.partial(spectra_kernel, segments, taps), grid_sp...  51.6 us
    all_to_all x2, starting transfers between devices, turn(): got = lax.all_to_all(spectra, ('ta', 'ba'), 0, 0, tiled=True)  20.2 us
    pallas_call x1, Pallas kernels, filter_part(): pl.pallas_call(functools.partial(partial_kernel, segments, taps), grid=(S...  17.7 us
    pallas_call x1, Pallas kernels, correlate(): pl.pallas_call(functools.partial(correlate_kernel, scale), in_specs=[pl.B...  9.42 us
    pallas_call x1, Pallas kernels, correlate(): pl.pallas_call(sums_kernel, grid=(channels,), in_specs=[pl.BlockSpec((tim...  7.83 us
    pallas_call x2, Pallas kernels, calibrate(): pl.pallas_call(calibrate_kernel, grid=(CALIBRATE_STEPS,), in_specs=[pl.Bl...  6.55 us
  transfers between devices with their start and end apart: 4, of which 3 were waited for; matrix products, arithmetic and copies ran while one was open for 0% of the time, Pallas kernels for 46%

profile of v4, /device:TPU:4, one launch (start us, length us, event | category | flops | bytes accessed | tf_op | source)
XLA Modules:
  0.0 175.6 jit_solution(14072673257625755075)
XLA Ops:
  0.0 3.4 %shard_map.55 = bf16[8,1024,128]{2,1,0:T(8,128)(2,1)} custom-call(s32[32,1024,128]{2,1,0:T(8,128)} %bitcast.6, f32[1,128]{1,0:T(1,128)} %bitcast.10), custom_call_target="tpu_custom_call" | custom-call | tf_op jit(solution)/shard_map/pallas_call | solution.py:35
  3.4 0.0 copy-start.1
  3.4 3.2 %collective-permute-start = (bf16[8,1024,128]{2,1,0:T(8,128)(2,1)}, bf16[8,1024,128]{2,1,0:T(8,128)(2,1)}, u32[]{:S(2)}, u32[]{:S(2)}) collective-permute-start(bf16[8,1024,128]{2,1,0:T(8,128)(2,1)} %shard_map.55), channel_id=1, source_target_pairs={{0,4},{4,8},{8,12},{12,16},{16,20},{20,24},{24,28},{28,32},{32,36}... | collective-permute-start | bytes 6291464 | tf_op jit(solution)/shard_map/ppermute | solution.py:321
  6.6 3.2 %shard_map.57 = bf16[7,1024,128]{2,1,0:T(8,128)(2,1)} custom-call(s32[32,1024,128]{2,1,0:T(8,128)} %bitcast.7, f32[1,128]{1,0:T(1,128)} %bitcast.11), custom_call_target="tpu_custom_call" | custom-call | tf_op jit(solution)/shard_map/pallas_call | solution.py:35
  9.8 0.8 collective-permute-start.1
  10.6 0.0 copy-done.1
  10.6 0.6 pad_maximum_fusion.scale_ref.refs_1_.refs_0_
  11.2 29.3 %shard_map.59 = bf16[128,8,16,128]{3,2,1,0:T(8,128)(2,1)} custom-call(s32[512]{0:T(512)} %chan_ref.3, s32[32,1024,128]{2,1,0:T(8,128)} %bitcast.8, f32[2,128]{1,0:T(2,128)} %pad_maximum_fusion.scale_ref.refs_1_.refs_0_, f32[16,1024]{1,0:T(8,128)} %refs_1_.1, bf16[1024,1024]{1,0:T(8,128)(2,1)} %constant.12.clone.refs_3_.refs_2_), custom_call_target="tpu_custom_call" | custom-call | flops 73014444032 | bytes 20971520 | tf_op jit(solution)/shard_map/pallas_call | solution.py:197
  40.5 11.5 %all-to-all-start.1 = ((bf16[128,8,16,128]{3,2,1,0:T(8,128)(2,1)}), bf16[128,8,16,128]{3,2,1,0:T(8,128)(2,1)}, u32[]{:S(2)}, u32[]{:S(2)}) async-start(bf16[128,8,16,128]{3,2,1,0:T(8,128)(2,1)} %shard_map.59), calls=%async_computation.1 | async-start | bytes 8388608 | tf_op jit(solution)/shard_map/all_to_all | solution.py:334
  52.0 2.3 %collective-permute-done.halo_ref = bf16[8,1024,128]{2,1,0:T(8,128)(2,1)} collective-permute-done((bf16[8,1024,128]{2,1,0:T(8,128)(2,1)}, bf16[8,1024,128]{2,1,0:T(8,128)(2,1)}, u32[]{:S(2)}, u32[]{:S(2)}) %collective-permute-start) | collective-permute-done | bytes 2097184 | tf_op jit(solution)/shard_map/ppermute | solution.py:321
  54.3 17.7 %shard_map.56.source_ref = f32[16,1024,128]{2,1,0:T(8,128)} custom-call(s32[32,1024,128]{2,1,0:T(8,128)} %bitcast.9, bf16[8,1024,128]{2,1,0:T(8,128)(2,1)} %collective-permute-done.halo_ref, f32[2,128]{1,0:T(2,128)} %pad_maximum_fusion.scale_ref.refs_1_.refs_0_, f32[16,1024]{1,0:T(8,128)} %refs_1_.1), custom_call_target="tpu_custom_call" | custom-call | flops 68719476736 | bytes 25165824 | tf_op jit(solution)/shard_map/pallas_call | solution.py:100
  72.1 0.0 collective-permute-done.1.refs_0_
  72.1 0.0 copy-start
  72.1 1.3 copy-done
  73.3 22.3 %shard_map.58 = bf16[128,8,16,128]{3,2,1,0:T(8,128)(2,1)} custom-call(s32[512]{0:T(512)} %chan_ref.3, f32[16,1024,128]{2,1,0:T(8,128)} %shard_map.56.source_ref, bf16[7,1024,128]{2,1,0:T(8,128)(2,1)} %copy-done, f32[2,128]{1,0:T(2,128)} %pad_maximum_fusion.scale_ref.refs_1_.refs_0_, f32[16,1024]{1,0:T(8,128)} %refs_1_.1, ...), custom_call_target="tpu_custom_call" | custom-call | flops 4294967296 | bytes 12582912 | tf_op jit(solution)/shard_map/pallas_call | solution.py:197
  95.6 9.1 %all-to-all-done.1 = bf16[128,8,16,128]{3,2,1,0:T(8,128)(2,1)} async-done(((bf16[128,8,16,128]{3,2,1,0:T(8,128)(2,1)}), bf16[128,8,16,128]{3,2,1,0:T(8,128)(2,1)}, u32[]{:S(2)}, u32[]{:S(2)}) %all-to-all-start.1) | async-done | bytes 4194336 | tf_op jit(solution)/shard_map/all_to_all | solution.py:334
  104.8 8.7 %all-to-all-start = ((bf16[128,8,16,128]{3,2,1,0:T(8,128)(2,1)}), bf16[128,8,16,128]{3,2,1,0:T(8,128)(2,1)}, u32[]{:S(2)}, u32[]{:S(2)}) async-start(bf16[128,8,16,128]{3,2,1,0:T(8,128)(2,1)} %shard_map.58), calls=%async_computation | async-start | bytes 8388608 | tf_op jit(solution)/shard_map/all_to_all | solution.py:334
  113.4 7.8 %shard_map.60.before_hbm = f32[4,512,512]{2,1,0:T(8,128)} custom-call(bf16[32,4,4,2,16,128]{5,4,3,2,1,0:T(8,128)(2,1)} %bitcast.4.cells_ref), custom_call_target="tpu_custom_call" | custom-call | flops 4294967296 | bytes 12582912 | tf_op jit(solution)/shard_map/pallas_call | solution.py:277
  121.3 44.9 %all-to-all-done = bf16[128,8,16,128]{3,2,1,0:T(8,128)(2,1)} async-done(((bf16[128,8,16,128]{3,2,1,0:T(8,128)(2,1)}), bf16[128,8,16,128]{3,2,1,0:T(8,128)(2,1)}, u32[]{:S(2)}, u32[]{:S(2)}) %all-to-all-start) | async-done | bytes 4194336 | tf_op jit(solution)/shard_map/all_to_all | solution.py:334
  166.2 9.4 %shard_map.61 = f32[2,4,512,512]{3,2,1,0:T(8,128)} custom-call(bf16[32,4,4,2,16,128]{5,4,3,2,1,0:T(8,128)(2,1)} %bitcast.3.cells_hbm, f32[4,512,512]{2,1,0:T(8,128)} %shard_map.60.before_hbm), custom_call_target="tpu_custom_call" | custom-call | flops 4294967296 | bytes 12582912 | tf_op jit(solution)/shard_map/pallas_call | solution.py:288
  (1 shorter events, 0.0 us)
Async XLA Ops:
  3.4 7.2 %copy-start.1 = (f32[128]{0:T(128)S(1)}, f32[128]{0:T(128)}, u32[]{:S(2)}) copy-start(f32[128]{0:T(128)} %param.6) | copy-start | bytes 1540
  3.4 51.0 %collective-permute-start = (bf16[8,1024,128]{2,1,0:T(8,128)(2,1)}, bf16[8,1024,128]{2,1,0:T(8,128)(2,1)}, u32[]{:S(2)}, u32[]{:S(2)}) collective-permute-start(bf16[8,1024,128]{2,1,0:T(8,128)(2,1)} %shard_map.55), channel_id=1, source_target_pairs={{0,4},{4,8},{8,12},{12,16},{16,20},{20,24},{24,28},{28,32},{32,36}... | collective-permute-start | bytes 6291464 | tf_op jit(solution)/shard_map/ppermute | solution.py:321
  9.8 62.3 %collective-permute-start.1 = (bf16[7,1024,128]{2,1,0:T(8,128)(2,1)}, bf16[7,1024,128]{2,1,0:T(8,128)(2,1)S(1)}, u32[]{:S(2)}, u32[]{:S(2)}) collective-permute-start(bf16[7,1024,128]{2,1,0:T(8,128)(2,1)} %shard_map.57), channel_id=1, source_target_pairs={{0,124},{4,0},{8,4},{12,8},{16,12},{20,16},{24,20},{28,24},{32,28}... | collective-permute-start | bytes 5505032 | tf_op jit(solution)/shard_map/ppermute | solution.py:320
  40.5 64.3 %all-to-all-start.1 = ((bf16[128,8,16,128]{3,2,1,0:T(8,128)(2,1)}), bf16[128,8,16,128]{3,2,1,0:T(8,128)(2,1)}, u32[]{:S(2)}, u32[]{:S(2)}) async-start(bf16[128,8,16,128]{3,2,1,0:T(8,128)(2,1)} %shard_map.59), calls=%async_computation.1 | async-start | bytes 8388608 | tf_op jit(solution)/shard_map/all_to_all | solution.py:334
  72.1 1.3 copy-start
  104.8 61.4 %all-to-all-start = ((bf16[128,8,16,128]{3,2,1,0:T(8,128)(2,1)}), bf16[128,8,16,128]{3,2,1,0:T(8,128)(2,1)}, u32[]{:S(2)}, u32[]{:S(2)}) async-start(bf16[128,8,16,128]{3,2,1,0:T(8,128)(2,1)} %shard_map.58), calls=%async_computation | async-start | bytes 8388608 | tf_op jit(solution)/shard_map/all_to_all | solution.py:334

commit v5 on v4

--- a/solution.py
+++ b/solution.py
@@ -13,7 +13,7 @@
 ROWS = 16
 STEPS = 8
 CALIBRATE_STEPS = 2
-VMEM = 60 * 1024 * 1024
+VMEM = 48 * 1024 * 1024
 FILTER_COST = 1024
 
 

time: 176 us -> 176 us (level)
  Pallas kernels: 93.1 us -> 89.8 us
  waiting for transfers between devices: 56.3 us -> 59.1 us
    ppermute x1, waiting for transfers between devices: 2.34 us -> 5.35 us  [per_device(): history = lax.ppermute(tail, 'ta', [(i, i + 1) for i in range(times - 1)])]
    pallas_call x2, Pallas kernels: 51.6 us -> 49.6 us  [transform(): pl.pallas_call(functools.partial(spectra_kernel, segments, taps), grid_sp...]
  transfers between devices with their start and end apart: 4 -> 4, of which waited for: 3 -> 3; matrix products, arithmetic and copies ran while one was open for 0% -> 0% of each run, Pallas kernels for 46% -> 44%
where the time goes in v5:
time: 176 us
  Pallas kernels  89.8 us (51%)
  waiting for transfers between devices  59.1 us (34%)
  starting transfers between devices  24 us (14%)
  local copies, waits for them, and re-layouts  2.62 us (1%)
    all_to_all x2, waiting for transfers between devices, turn(): got = lax.all_to_all(spectra, ('ta', 'ba'), 0, 0, tiled=True)  53.7 us
    pallas_call x2, Pallas kernels, transform(): pl.pallas_call(functools.partial(spectra_kernel, segments, taps), grid_sp...  49.6 us
    all_to_all x2, starting transfers between devices, turn(): got = lax.all_to_all(spectra, ('ta', 'ba'), 0, 0, tiled=True)  19.9 us
    pallas_call x1, Pallas kernels, filter_part(): pl.pallas_call(functools.partial(partial_kernel, segments, taps), grid=(S...  17.7 us
    pallas_call x1, Pallas kernels, correlate(): pl.pallas_call(functools.partial(correlate_kernel, scale), in_specs=[pl.B...  9.42 us
    pallas_call x2, Pallas kernels, calibrate(): pl.pallas_call(calibrate_kernel, grid=(CALIBRATE_STEPS,), in_specs=[pl.Bl...  6.55 us
    pallas_call x1, Pallas kernels, correlate(): pl.pallas_call(sums_kernel, grid=(channels,), in_specs=[pl.BlockSpec((tim...  6.48 us
    ppermute x1, waiting for transfers between devices, per_device(): history = lax.ppermute(tail, 'ta', [(i, i + 1) for i in range(times - 1)])  5.35 us
  transfers between devices with their start and end apart: 4, of which 3 were waited for; matrix products, arithmetic and copies ran while one was open for 0% of the time, Pallas kernels for 44%

profile of v5, /device:TPU:4, one launch (start us, length us, event | category | flops | bytes accessed | tf_op | source)
XLA Modules:
  0.0 175.5 jit_solution(7547631260253501922)
XLA Ops:
  0.0 0.0 copy-start.3
  0.0 0.7 copy-done.3
  0.7 3.4 %shard_map.55 = bf16[8,1024,128]{2,1,0:T(8,128)(2,1)} custom-call(s32[32,1024,128]{2,1,0:T(8,128)} %bitcast.9, f32[1,128]{1,0:T(1,128)S(1)} %bitcast.6), custom_call_target="tpu_custom_call" | custom-call | tf_op jit(solution)/shard_map/pallas_call | solution.py:35
  4.0 0.0 copy-start.4
  4.0 0.0 copy-start.1
  4.0 0.0 copy-start.2
  4.0 0.0 copy-start.5
  4.0 3.2 %collective-permute-start = (bf16[8,1024,128]{2,1,0:T(8,128)(2,1)}, bf16[8,1024,128]{2,1,0:T(8,128)(2,1)}, u32[]{:S(2)}, u32[]{:S(2)}) collective-permute-start(bf16[8,1024,128]{2,1,0:T(8,128)(2,1)} %shard_map.55), channel_id=1, source_target_pairs={{0,4},{4,8},{8,12},{12,16},{16,20},{20,24},{24,28},{28,32},{32,36}... | collective-permute-start | bytes 6291464 | tf_op jit(solution)/shard_map/ppermute | solution.py:321
  7.3 3.2 %shard_map.57 = bf16[7,1024,128]{2,1,0:T(8,128)(2,1)} custom-call(s32[32,1024,128]{2,1,0:T(8,128)} %bitcast.10, f32[1,128]{1,0:T(1,128)S(1)} %bitcast.7), custom_call_target="tpu_custom_call" | custom-call | tf_op jit(solution)/shard_map/pallas_call | solution.py:35
  10.5 0.8 collective-permute-start.1
  11.3 0.0 copy-done.4
  11.3 0.0 copy-done.1
  11.3 0.0 copy-done.2
  11.3 0.0 copy-done.5
  11.3 28.3 %shard_map.59 = bf16[128,8,16,128]{3,2,1,0:T(8,128)(2,1)} custom-call(s32[512]{0:T(512)S(1)} %copy-done.5, s32[32,1024,128]{2,1,0:T(8,128)} %bitcast.11, f32[2,128]{1,0:T(2,128)S(1)} %pad_maximum_fusion.scale_ref.refs_1_.refs_0_, f32[16,1024]{1,0:T(8,128)S(1)} %copy-done.2, bf16[1024,1024]{1,0:T(8,128)(2,1)S(1)} %copy-done.1), custom_call_target="tpu_custom_call" | custom-call | flops 73014444032 | bytes 20971520 | tf_op jit(solution)/shard_map/pallas_call | solution.py:197
  39.7 11.5 %all-to-all-start.1 = ((bf16[128,8,16,128]{3,2,1,0:T(8,128)(2,1)}), bf16[128,8,16,128]{3,2,1,0:T(8,128)(2,1)}, u32[]{:S(2)}, u32[]{:S(2)}) async-start(bf16[128,8,16,128]{3,2,1,0:T(8,128)(2,1)} %shard_map.59), calls=%async_computation.1 | async-start | bytes 8388608 | tf_op jit(solution)/shard_map/all_to_all | solution.py:334
  51.2 5.4 %collective-permute-done.halo_ref = bf16[8,1024,128]{2,1,0:T(8,128)(2,1)} collective-permute-done((bf16[8,1024,128]{2,1,0:T(8,128)(2,1)}, bf16[8,1024,128]{2,1,0:T(8,128)(2,1)}, u32[]{:S(2)}, u32[]{:S(2)}) %collective-permute-start) | collective-permute-done | bytes 2097184 | tf_op jit(solution)/shard_map/ppermute | solution.py:321
  56.5 17.7 %shard_map.56.source_ref = f32[16,1024,128]{2,1,0:T(8,128)} custom-call(s32[32,1024,128]{2,1,0:T(8,128)} %bitcast.12, bf16[8,1024,128]{2,1,0:T(8,128)(2,1)} %collective-permute-done.halo_ref, f32[2,128]{1,0:T(2,128)S(1)} %pad_maximum_fusion.scale_ref.refs_1_.refs_0_, f32[16,1024]{1,0:T(8,128)S(1)} %copy-done.2), custom_call_target="tpu_custom_call" | custom-call | flops 68719476736 | bytes 25165824 | tf_op jit(solution)/shard_map/pallas_call | solution.py:100
  74.2 0.0 collective-permute-done.1.refs_0_
  74.2 21.3 %shard_map.58 = bf16[128,8,16,128]{3,2,1,0:T(8,128)(2,1)} custom-call(s32[512]{0:T(512)S(1)} %copy-done.5, f32[16,1024,128]{2,1,0:T(8,128)} %shard_map.56.source_ref, bf16[7,1024,128]{2,1,0:T(8,128)(2,1)} %collective-permute-done.1.refs_0_, f32[2,128]{1,0:T(2,128)S(1)} %pad_maximum_fusion.scale_ref.refs_1_.refs_0_, f32[16,1024]{1,0:T(8,128)S(1)} %copy-done.2, ...), custom_call_target="tpu_custom_call" | custom-call | flops 4294967296 | bytes 12582912 | tf_op jit(solution)/shard_map/pallas_call | solution.py:197
  95.5 9.4 %all-to-all-done.1 = bf16[128,8,16,128]{3,2,1,0:T(8,128)(2,1)} async-done(((bf16[128,8,16,128]{3,2,1,0:T(8,128)(2,1)}), bf16[128,8,16,128]{3,2,1,0:T(8,128)(2,1)}, u32[]{:S(2)}, u32[]{:S(2)}) %all-to-all-start.1) | async-done | bytes 4194336 | tf_op jit(solution)/shard_map/all_to_all | solution.py:334
  105.0 8.4 %all-to-all-start = ((bf16[128,8,16,128]{3,2,1,0:T(8,128)(2,1)}), bf16[128,8,16,128]{3,2,1,0:T(8,128)(2,1)}, u32[]{:S(2)}, u32[]{:S(2)}) async-start(bf16[128,8,16,128]{3,2,1,0:T(8,128)(2,1)} %shard_map.58), calls=%async_computation | async-start | bytes 8388608 | tf_op jit(solution)/shard_map/all_to_all | solution.py:334
  113.4 6.5 %shard_map.60.before_hbm = f32[4,512,512]{2,1,0:T(8,128)S(1)} custom-call(bf16[32,4,4,2,16,128]{5,4,3,2,1,0:T(8,128)(2,1)} %bitcast.4.cells_ref), custom_call_target="tpu_custom_call" | custom-call | flops 4294967296 | bytes 12582912 | tf_op jit(solution)/shard_map/pallas_call | solution.py:277
  119.9 0.0 copy-start
  119.9 1.9 %copy-done = f32[4,512,512]{2,1,0:T(8,128)} copy-done((f32[4,512,512]{2,1,0:T(8,128)}, f32[4,512,512]{2,1,0:T(8,128)S(1)}, u32[]{:S(2)}) %copy-start) | copy-done | bytes 4194328
  121.8 44.3 %all-to-all-done = bf16[128,8,16,128]{3,2,1,0:T(8,128)(2,1)} async-done(((bf16[128,8,16,128]{3,2,1,0:T(8,128)(2,1)}), bf16[128,8,16,128]{3,2,1,0:T(8,128)(2,1)}, u32[]{:S(2)}, u32[]{:S(2)}) %all-to-all-start) | async-done | bytes 4194336 | tf_op jit(solution)/shard_map/all_to_all | solution.py:334
  166.1 9.4 %shard_map.61 = f32[2,4,512,512]{3,2,1,0:T(8,128)} custom-call(bf16[32,4,4,2,16,128]{5,4,3,2,1,0:T(8,128)(2,1)} %bitcast.3.cells_hbm, f32[4,512,512]{2,1,0:T(8,128)} %copy-done), custom_call_target="tpu_custom_call" | custom-call | flops 4294967296 | bytes 12582912 | tf_op jit(solution)/shard_map/pallas_call | solution.py:288
  (2 shorter events, 0.0 us)
Async XLA Ops:
  0.0 0.7 copy-start.3
  4.0 7.3 %copy-start.4 = (f32[128]{0:T(128)S(1)}, f32[128]{0:T(128)}, u32[]{:S(2)}) copy-start(f32[128]{0:T(128)} %param.6) | copy-start | bytes 1540
  4.0 7.3 %copy-start.1 = (bf16[1024,1024]{1,0:T(8,128)(2,1)S(1)}, bf16[1024,1024]{1,0:T(8,128)(2,1)}, u32[]{:S(2)}) copy-start(bf16[1024,1024]{1,0:T(8,128)(2,1)} %constant.12.clone.refs_3_.refs_2_) | copy-start | bytes 6291460
  4.0 7.3 %copy-start.2 = (f32[16,1024]{1,0:T(8,128)S(1)}, f32[16,1024]{1,0:T(8,128)}, u32[]{:S(2)}) copy-start(f32[16,1024]{1,0:T(8,128)} %refs_1_.1) | copy-start | bytes 196612
  4.0 7.3 %copy-start.5 = (s32[512]{0:T(512)S(1)}, s32[512]{0:T(512)}, u32[]{:S(2)}) copy-start(s32[512]{0:T(512)} %chan_ref.3) | copy-start | bytes 6148
  4.0 52.5 %collective-permute-start = (bf16[8,1024,128]{2,1,0:T(8,128)(2,1)}, bf16[8,1024,128]{2,1,0:T(8,128)(2,1)}, u32[]{:S(2)}, u32[]{:S(2)}) collective-permute-start(bf16[8,1024,128]{2,1,0:T(8,128)(2,1)} %shard_map.55), channel_id=1, source_target_pairs={{0,4},{4,8},{8,12},{12,16},{16,20},{20,24},{24,28},{28,32},{32,36}... | collective-permute-start | bytes 6291464 | tf_op jit(solution)/shard_map/ppermute | solution.py:321
  10.5 63.8 %collective-permute-start.1 = (bf16[7,1024,128]{2,1,0:T(8,128)(2,1)}, bf16[7,1024,128]{2,1,0:T(8,128)(2,1)}, u32[]{:S(2)}, u32[]{:S(2)}) collective-permute-start(bf16[7,1024,128]{2,1,0:T(8,128)(2,1)} %shard_map.57), channel_id=1, source_target_pairs={{0,124},{4,0},{8,4},{12,8},{16,12},{20,16},{24,20},{28,24},{32,28}... | collective-permute-start | bytes 5505032 | tf_op jit(solution)/shard_map/ppermute | solution.py:320
  39.7 65.3 %all-to-all-start.1 = ((bf16[128,8,16,128]{3,2,1,0:T(8,128)(2,1)}), bf16[128,8,16,128]{3,2,1,0:T(8,128)(2,1)}, u32[]{:S(2)}, u32[]{:S(2)}) async-start(bf16[128,8,16,128]{3,2,1,0:T(8,128)(2,1)} %shard_map.59), calls=%async_computation.1 | async-start | bytes 8388608 | tf_op jit(solution)/shard_map/all_to_all | solution.py:334
  105.0 61.2 %all-to-all-start = ((bf16[128,8,16,128]{3,2,1,0:T(8,128)(2,1)}), bf16[128,8,16,128]{3,2,1,0:T(8,128)(2,1)}, u32[]{:S(2)}, u32[]{:S(2)}) async-start(bf16[128,8,16,128]{3,2,1,0:T(8,128)(2,1)} %shard_map.58), calls=%async_computation | async-start | bytes 8388608 | tf_op jit(solution)/shard_map/all_to_all | solution.py:334
  119.9 2.0 %copy-start = (f32[4,512,512]{2,1,0:T(8,128)}, f32[4,512,512]{2,1,0:T(8,128)S(1)}, u32[]{:S(2)}) copy-start(f32[4,512,512]{2,1,0:T(8,128)S(1)} %shard_map.60.before_hbm) | copy-start | bytes 12582916
